TPU v7x, 512 devices: a whole 4x4x16 slice. The times are simulated.
512 devices in a mesh: lat: 64 (over y, z), lon: 8 (over x, core).
Axes of the slice: x: 4, y: 4, z: 16, core: 2. Of those that a mesh axis runs over, the one named last changes fastest.
Arguments:
- covariance: float32 [64, 64, 128, 128], P('lat', None, 'lon'), may hold values from -6 to 6
- winds: float32 [2, 3, 64, 128], P(None, None, None, 'lon'), may hold values from -0.35 to 0.35
- diffusivity: float32 [64, 128], P(None, 'lon'), may hold values from 0.01 to 0.07
- cutoff: int32 [64], replicated, may hold values from 4 to 16, as said below
Outputs:
- forecast: float32 [64, 64, 128, 128], P('lat', None, 'lon')
Inputs may be any that keep to these rules, and one draw needn't show every extreme that they name: Some latitude has cutoff 16 and some other has 4.
All inputs are finite; a program needn't handle non-finite values.
Results may differ from a plain program's by a relative error of at most 0.00002.
Values sent between devices are 32-bit elements; how exact they have to be, the bound alone decides.
A program may use at most 192 MiB of HBM per device.

v0:
```python
import jax
import jax.numpy as jnp
from jax import lax
from jax.sharding import PartitionSpec as P

STEPS = 3


def extended_2(block, sides, width):
    for axis, dim in sides:
        count = lax.axis_size(axis)
        forward = [(i, i + 1) for i in range(count - 1)]
        forward.append((count - 1, 0))
        backward = [(target, source) for source, target in forward]
        low = lax.ppermute(
            lax.slice_in_dim(block, block.shape[dim] - width, None, axis=dim), axis, forward
        )
        high = lax.ppermute(lax.slice_in_dim(block, 0, width, axis=dim), axis, backward)
        block = jnp.concatenate([low, block, high], axis=dim)
    return block


def from_behind(shard, axis, by):
    length = lax.axis_size(axis)
    pairs = [(i, i + by) for i in range(length) if 0 <= i + by < length]
    return lax.ppermute(shard, axis, pairs)


def advance(extended, east_wind, north_wind, spread):
    center = extended[:, :, 1:-1]
    western = extended[:, :, :-2]
    eastern = extended[:, :, 2:]
    zeros_row = jnp.zeros_like(center[:, :1])
    southern = jnp.concatenate([zeros_row, center[:, :-1]], axis=1)
    northern = jnp.concatenate([center[:, 1:], zeros_row], axis=1)
    east_wind = east_wind[None, :, :, None]
    north_wind = north_wind[None, :, :, None]
    spread = spread[None, :, :, None]
    transport = (
        jnp.maximum(east_wind, 0.0) * (center - western)
        + jnp.minimum(east_wind, 0.0) * (eastern - center)
        + jnp.maximum(north_wind, 0.0) * (center - southern)
        + jnp.minimum(north_wind, 0.0) * (northern - center)
    )
    return center - transport + spread * (eastern + western + northern + southern - 4.0 * center)


def propagate(state_field, winds, diffusivity):
    for substep in range(STEPS):
        extended = extended_2(state_field, (("lon", 2),), 1)
        state_field = advance(extended, winds[0, substep], winds[1, substep], diffusivity)
    return state_field


def relayout(block, reach_rows):
    row_count = block.shape[0]
    lat_count = block.shape[1]
    swapped = lax.all_to_all(block, "lon", split_axis=3, concat_axis=2, tiled=True)
    lon_count = swapped.shape[2]
    col_count = swapped.shape[3]
    block_count = lat_count // row_count
    device_index = lax.axis_index("lat")
    reach_blocks = min((reach_rows + row_count - 1) // row_count, block_count - 1)
    tile_blocks = swapped.reshape(row_count, block_count, row_count, lon_count, col_count)

    def piece_for(offset):
        target = jnp.clip(device_index + offset, 0, block_count - 1)
        return lax.dynamic_index_in_dim(tile_blocks, target, axis=1, keepdims=False)

    own_piece = piece_for(0)
    received = []
    for offset in range(-reach_blocks, reach_blocks + 1):
        if offset == 0:
            received.append(own_piece)
        else:
            received.append(from_behind(piece_for(offset), "lat", offset))
    window = jnp.stack(received[::-1], axis=0)
    padded = jnp.zeros(
        (block_count + 2 * reach_blocks, row_count, row_count, lon_count, col_count), jnp.float32
    )
    padded = lax.dynamic_update_slice_in_dim(padded, window, device_index, 0)
    regrouped = padded[reach_blocks : reach_blocks + block_count].reshape(
        lat_count, row_count, lon_count, col_count
    )
    return jnp.transpose(regrouped, (1, 0, 3, 2))


def per_device(covariance, winds, diffusivity, cutoff):
    row_count = covariance.shape[0]
    lat_count = covariance.shape[1]
    band_rows = lat_count // 4
    device_index = lax.axis_index("lat")
    lat_local = device_index * row_count + jnp.arange(row_count, dtype=jnp.int32)
    lat_all = jnp.arange(lat_count, dtype=jnp.int32)
    cut_local = lax.dynamic_slice_in_dim(cutoff, device_index * row_count, row_count)
    keep_first = jnp.abs(lat_all[None, :] - lat_local[:, None]) <= cutoff[None, :]
    keep_second = jnp.abs(lat_all[None, :] - lat_local[:, None]) <= cut_local[:, None]
    state_field = jnp.where(keep_first[:, :, None, None], covariance, 0.0)
    state_field = propagate(state_field, winds, diffusivity)
    state_field = relayout(state_field, band_rows + STEPS)
    state_field = propagate(state_field, winds, diffusivity)
    state_field = jnp.where(keep_second[:, :, None, None], state_field, 0.0)
    return relayout(state_field, band_rows)


def solution(mesh):
    in_specs = (P("lat", None, "lon", None), P(None, None, None, "lon"), P(None, "lon"), P())
    out_specs = P("lat", None, "lon", None)
    return jax.shard_map(
        per_device, mesh=mesh, in_specs=in_specs, out_specs=out_specs, check_vma=False
    )
```

profile of v0, /device:TPU:24, one launch (start us, length us, event | category | flops | bytes accessed | tf_op | source)
XLA Modules:
  0.0 880.4 jit_solution(16110254045664270610)
XLA Ops:
  2.5 2.9 collective-permute-start.1
  9.7 2.6 collective-permute-start.3
  16.1 3.0 collective-permute-start.5
  24.3 4.2 all-to-all-start
  28.5 10.3 %all-to-all-done = f32[8,1,16384]{2,1,0:T(1,128)S(1)} async-done(((f32[8,1,16384]{2,1,0:T(1,128)}), f32[8,1,16384]{2,1,0:T(1,128)S(1)}, u32[]{:S(2)}, u32[]{:S(2)}) %all-to-all-start) | async-done | bytes 524320 | tf_op jit(solution)/shard_map/all_to_all | solution.py:58
  44.4 8.4 constant_dynamic-slice_fusion.51
  54.4 21.2 %collective-permute-start.7 = (f32[1,1,128,16]{2,3,1,0:T(8,128)S(1)}, f32[1,1,128,16]{2,3,1,0:T(8,128)S(1)}, u32[]{:S(2)}, u32[]{:S(2)}) collective-permute-start(f32[1,1,128,16]{2,3,1,0:T(8,128)S(1)} %bitcast.330), channel_id=1, source_target_pairs={{0,144},{8,152},{16,160},{24,168},{32,176},{40,184},{48,192},{56,2... | collective-permute-start | bytes 24584 | tf_op jit(solution)/shard_map/ppermute | solution.py:26
  77.3 19.0 %collective-permute-start.8 = (f32[1,1,128,16]{2,3,1,0:T(8,128)S(1)}, f32[1,1,128,16]{2,3,1,0:T(8,128)S(1)}, u32[]{:S(2)}, u32[]{:S(2)}) collective-permute-start(f32[1,1,128,16]{2,3,1,0:T(8,128)S(1)} %bitcast.329), channel_id=1, source_target_pairs={{0,136},{8,144},{16,152},{24,160},{32,168},{40,176},{48,184},{56,1... | collective-permute-start | bytes 24584 | tf_op jit(solution)/shard_map/ppermute | solution.py:26
  100.8 8.6 collective-permute-start.10
  130.2 3.1 collective-permute-start.14
  139.1 4.8 collective-permute-start.18
  143.9 8.9 %constant_dynamic-slice_fusion.32 = (f32[1,1,1,128,16]{1,4,3,2,0:T(8,128)}, f32[1,1,1,128,16]{1,4,3,2,0:T(8,128)}, f32[1,1,1,128,16]{1,4,3,2,0:T(8,128)}, f32[1,...) fusion(f32[1,64,1,128,16]{1,4,3,2,0:T(8,128)S(1)} %bitcast.189,, ...), kind=kLoop, calls=%fused_computation.205 | loop fusion | bytes 294984 | tf_op jit(solution)/shard_map/jit(dynamic_index_in_dim)/dynamic_slice | solution.py:68
  197.3 2.5 collective-permute-start.22
  218.0 2.5 collective-permute-start.24
  222.6 6.4 collective-permute-start.26
  231.1 6.9 collective-permute-start.27
  239.4 7.8 collective-permute-start.28
  248.6 8.7 collective-permute-start.29
  263.3 2.3 constant_dynamic-update-slice_fusion.34
  270.2 2.4 constant_dynamic-update-slice_fusion.31
  272.5 2.3 constant_dynamic-update-slice_fusion.30
  292.9 2.3 constant_dynamic-update-slice_fusion.20
  295.2 10.0 %collective-permute-start.30 = (f32[1,1,128,16]{2,3,1,0:T(8,128)S(1)}, f32[1,1,128,16]{2,3,1,0:T(8,128)S(1)}, u32[]{:S(2)}, u32[]{:S(2)}) collective-permute-start(f32[1,1,128,16]{2,3,1,0:T(8,128)S(1)} %bitcast.218), channel_id=1, source_target_pairs={{48,0},{56,8},{64,16},{72,24},{80,32},{88,40},{96,48},{104,56},{11... | collective-permute-start | bytes 24584 | tf_op jit(solution)/shard_map/ppermute | solution.py:26
  305.7 11.5 %collective-permute-start.31 = (f32[1,1,128,16]{2,3,1,0:T(8,128)S(1)}, f32[1,1,128,16]{2,3,1,0:T(8,128)S(1)}, u32[]{:S(2)}, u32[]{:S(2)}) collective-permute-start(f32[1,1,128,16]{2,3,1,0:T(8,128)S(1)} %bitcast.217), channel_id=1, source_target_pairs={{56,0},{64,8},{72,16},{80,24},{88,32},{96,40},{104,48},{112,56},{1... | collective-permute-start | bytes 24584 | tf_op jit(solution)/shard_map/ppermute | solution.py:26
  317.2 12.4 %collective-permute-start.32 = (f32[1,1,128,16]{2,3,1,0:T(8,128)S(1)}, f32[1,1,128,16]{2,3,1,0:T(8,128)S(1)}, u32[]{:S(2)}, u32[]{:S(2)}) collective-permute-start(f32[1,1,128,16]{2,3,1,0:T(8,128)S(1)} %bitcast.216), channel_id=1, source_target_pairs={{64,0},{72,8},{80,16},{88,24},{96,32},{104,40},{112,48},{120,56},{... | collective-permute-start | bytes 24584 | tf_op jit(solution)/shard_map/ppermute | solution.py:26
  329.6 10.3 %collective-permute-start.33 = (f32[1,1,128,16]{2,3,1,0:T(8,128)S(1)}, f32[1,1,128,16]{2,3,1,0:T(8,128)S(1)}, u32[]{:S(2)}, u32[]{:S(2)}) collective-permute-start(f32[1,1,128,16]{2,3,1,0:T(8,128)S(1)} %bitcast.215), channel_id=1, source_target_pairs={{72,0},{80,8},{88,16},{96,24},{104,32},{112,40},{120,48},{128,56},... | collective-permute-start | bytes 24584 | tf_op jit(solution)/shard_map/ppermute | solution.py:26
  340.0 2.7 collective-permute-start.34
  357.7 13.2 %collective-permute-start.41 = (f32[1,1,128,16]{2,3,1,0:T(8,128)S(1)}, f32[1,1,128,16]{2,3,1,0:T(8,128)S(1)}, u32[]{:S(2)}, u32[]{:S(2)}) collective-permute-start(f32[1,1,128,16]{2,3,1,0:T(8,128)S(1)} %bitcast.199), channel_id=1, source_target_pairs={{136,0},{144,8},{152,16},{160,24},{168,32},{176,40},{184,48},{192,... | collective-permute-start | bytes 24584 | tf_op jit(solution)/shard_map/ppermute | solution.py:26
  371.0 19.0 %collective-permute-start.42 = (f32[1,1,128,16]{2,3,1,0:T(8,128)S(1)}, f32[1,1,128,16]{2,3,1,0:T(8,128)S(1)}, u32[]{:S(2)}, u32[]{:S(2)}) collective-permute-start(f32[1,1,128,16]{2,3,1,0:T(8,128)S(1)} %bitcast.198), channel_id=1, source_target_pairs={{144,0},{152,8},{160,16},{168,24},{176,32},{184,40},{192,48},{200,... | collective-permute-start | bytes 24584 | tf_op jit(solution)/shard_map/ppermute | solution.py:26
  390.0 19.0 %collective-permute-start.43 = (f32[1,1,128,16]{2,3,1,0:T(8,128)S(1)}, f32[1,1,128,16]{2,3,1,0:T(8,128)S(1)}, u32[]{:S(2)}, u32[]{:S(2)}) collective-permute-start(f32[1,1,128,16]{2,3,1,0:T(8,128)S(1)} %bitcast.197), channel_id=1, source_target_pairs={{152,0},{160,8},{168,16},{176,24},{184,32},{192,40},{200,48},{208,... | collective-permute-start | bytes 24584 | tf_op jit(solution)/shard_map/ppermute | solution.py:26
  409.0 9.1 %collective-permute-start.25 = (f32[1,1,128,16]{2,3,1,0:T(8,128)S(1)}, f32[1,1,128,16]{2,3,1,0:T(8,128)S(1)}, u32[]{:S(2)}, u32[]{:S(2)}) collective-permute-start(f32[1,1,128,16]{2,3,1,0:T(8,128)S(1)} %bitcast.265), channel_id=1, source_target_pairs={{8,0},{16,8},{24,16},{32,24},{40,32},{48,40},{56,48},{64,56},{72,6... | collective-permute-start | bytes 24584 | tf_op jit(solution)/shard_map/ppermute | solution.py:26
  447.5 2.4 constant_dynamic-update-slice_fusion.16
  449.9 2.3 constant_dynamic-update-slice_fusion.15
  480.4 2.3 constant_dynamic-update-slice_fusion
  482.8 23.8 %copy.588 = f32[39,1,1,128,16]{0,4,3,2,1:T(8,128)S(1)} copy(f32[39,1,1,128,16]{1,4,3,2,0:T(8,128)} %constant_dynamic-update-slice_fusion) | data formatting | bytes 638976 | tf_op jit(solution)/shard_map/stack | solution.py:77
  506.6 21.2 %dynamic_update_slice.6 = f32[102,1,1,128,16]{0,4,3,2,1:T(8,128)S(1)} dynamic-update-slice(f32[102,1,1,128,16]{0,4,3,2,1:T(8,128)S(1)} %broadcast_in_dim.38, f32[39,1,1,128,16]{0,4,3,2,1:T(8,128)S(1)} %copy.588, s32[]{:T(128)S(6)} %select_n.91, s32[]{:T(128)} %constant.241.clone.1, s32[]{:T(128)} %constant.241.clone.1, s32[]{:T(128)} %constant.241.clone.1, s32[]{:T(128)} %constant.241.clone.1) | dynamic-update-slice | bytes 638980 | tf_op jit(solution)/shard_map/dynamic_update_slice | solution.py:81
  528.3 2.9 collective-permute-start.45
  534.8 2.6 collective-permute-start.47
  540.5 3.0 collective-permute-start.49
  547.2 14.6 %all_to_all.30 = f32[8,1,16384]{2,1,0:T(1,128)S(1)} all-to-all(f32[8,1,16384]{2,1,0:T(1,128)S(1)} %reshape.178), channel_id=1, replica_groups=mesh['lat'=64,'lon'=8] {'lon'}, dimensions={0} | all-to-all | bytes 1048576 | tf_op jit(solution)/shard_map/all_to_all | solution.py:58
  564.6 7.4 constant_dynamic-slice_fusion.16
  576.6 2.9 collective-permute-start.51
  588.2 3.1 collective-permute-start.54
  608.8 4.4 collective-permute-start.59
  623.4 2.3 collective-permute-start.62
  629.8 2.7 collective-permute-start.65
  657.6 2.3 constant_dynamic-update-slice_fusion.66
  664.4 2.4 constant_dynamic-update-slice_fusion.63
  666.8 2.3 constant_dynamic-update-slice_fusion.62
  684.9 7.9 constant_dynamic-slice_fusion
  694.4 5.5 collective-permute-start.66
  701.5 4.8 collective-permute-start.67
  707.9 6.8 collective-permute-start.68
  716.4 7.4 collective-permute-start.69
  725.4 8.7 collective-permute-start.70
  735.8 12.0 %collective-permute-start.71 = (f32[1,1,128,16]{2,3,1,0:T(8,128)S(1)}, f32[1,1,128,16]{2,3,1,0:T(8,128)S(1)}, u32[]{:S(2)}, u32[]{:S(2)}) collective-permute-start(f32[1,1,128,16]{2,3,1,0:T(8,128)S(1)} %bitcast.320), channel_id=1, source_target_pairs={{48,0},{56,8},{64,16},{72,24},{80,32},{88,40},{96,48},{104,56},{11... | collective-permute-start | bytes 24584 | tf_op jit(solution)/shard_map/ppermute | solution.py:26
  755.9 9.7 %collective-permute-start.72 = (f32[1,1,128,16]{2,3,1,0:T(8,128)S(1)}, f32[1,1,128,16]{2,3,1,0:T(8,128)S(1)}, u32[]{:S(2)}, u32[]{:S(2)}) collective-permute-start(f32[1,1,128,16]{2,3,1,0:T(8,128)S(1)} %bitcast.311), channel_id=1, source_target_pairs={{56,0},{64,8},{72,16},{80,24},{88,32},{96,40},{104,48},{112,56},{1... | collective-permute-start | bytes 24584 | tf_op jit(solution)/shard_map/ppermute | solution.py:26
  765.6 12.4 %collective-permute-start.73 = (f32[1,1,128,16]{2,3,1,0:T(8,128)S(1)}, f32[1,1,128,16]{2,3,1,0:T(8,128)S(1)}, u32[]{:S(2)}, u32[]{:S(2)}) collective-permute-start(f32[1,1,128,16]{2,3,1,0:T(8,128)S(1)} %bitcast.304), channel_id=1, source_target_pairs={{64,0},{72,8},{80,16},{88,24},{96,32},{104,40},{112,48},{120,56},{... | collective-permute-start | bytes 24584 | tf_op jit(solution)/shard_map/ppermute | solution.py:26
  778.0 10.1 %collective-permute-start.74 = (f32[1,1,128,16]{2,3,1,0:T(8,128)S(1)}, f32[1,1,128,16]{2,3,1,0:T(8,128)S(1)}, u32[]{:S(2)}, u32[]{:S(2)}) collective-permute-start(f32[1,1,128,16]{2,3,1,0:T(8,128)S(1)} %bitcast.299), channel_id=1, source_target_pairs={{72,0},{80,8},{88,16},{96,24},{104,32},{112,40},{120,48},{128,56},... | collective-permute-start | bytes 24584 | tf_op jit(solution)/shard_map/ppermute | solution.py:26
  827.0 2.3 constant_dynamic-update-slice_fusion.53
  831.6 2.3 constant_dynamic-update-slice_fusion.51
  838.4 2.4 constant_dynamic-update-slice_fusion.48
  840.8 2.3 constant_dynamic-update-slice_fusion.47
  860.0 19.0 %copy.655 = f32[33,1,1,128,16]{3,4,0,2,1:T(8,128)S(1)} copy(f32[33,1,1,128,16]{1,4,3,2,0:T(8,128)} %constant_dynamic-update-slice_fusion.38) | data formatting | bytes 540672 | tf_op jit(solution)/shard_map/stack | solution.py:77
  (366 shorter events, 411.7 us)
Async XLA Ops:
  42.9 71.4 %collective-permute-start.6 = (f32[1,1,128,16]{2,3,1,0:T(8,128)S(1)}, f32[1,1,128,16]{2,3,1,0:T(8,128)S(1)}, u32[]{:S(2)}, u32[]{:S(2)}) collective-permute-start(f32[1,1,128,16]{2,3,1,0:T(8,128)S(1)} %bitcast.315), channel_id=1, source_target_pairs={{0,152},{8,160},{16,168},{24,176},{32,184},{40,192},{48,200},{56,2... | collective-permute-start | bytes 24584 | tf_op jit(solution)/shard_map/ppermute | solution.py:26
  54.4 61.8 %collective-permute-start.7 = (f32[1,1,128,16]{2,3,1,0:T(8,128)S(1)}, f32[1,1,128,16]{2,3,1,0:T(8,128)S(1)}, u32[]{:S(2)}, u32[]{:S(2)}) collective-permute-start(f32[1,1,128,16]{2,3,1,0:T(8,128)S(1)} %bitcast.330), channel_id=1, source_target_pairs={{0,144},{8,152},{16,160},{24,168},{32,176},{40,184},{48,192},{56,2... | collective-permute-start | bytes 24584 | tf_op jit(solution)/shard_map/ppermute | solution.py:26
  77.3 40.9 %collective-permute-start.8 = (f32[1,1,128,16]{2,3,1,0:T(8,128)S(1)}, f32[1,1,128,16]{2,3,1,0:T(8,128)S(1)}, u32[]{:S(2)}, u32[]{:S(2)}) collective-permute-start(f32[1,1,128,16]{2,3,1,0:T(8,128)S(1)} %bitcast.329), channel_id=1, source_target_pairs={{0,136},{8,144},{16,152},{24,160},{32,168},{40,176},{48,184},{56,1... | collective-permute-start | bytes 24584 | tf_op jit(solution)/shard_map/ppermute | solution.py:26
  97.9 32.3 %collective-permute-start.9 = (f32[1,1,128,16]{2,3,1,0:T(8,128)S(1)}, f32[1,1,128,16]{2,3,1,0:T(8,128)S(1)}, u32[]{:S(2)}, u32[]{:S(2)}) collective-permute-start(f32[1,1,128,16]{2,3,1,0:T(8,128)S(1)} %bitcast.232), channel_id=1, source_target_pairs={{0,128},{8,136},{16,144},{24,152},{32,160},{40,168},{48,176},{56,1... | collective-permute-start | bytes 24584 | tf_op jit(solution)/shard_map/ppermute | solution.py:26
  100.8 32.5 %collective-permute-start.10 = (f32[1,1,128,16]{2,3,1,0:T(8,128)S(1)}, f32[1,1,128,16]{2,3,1,0:T(8,128)S(1)}, u32[]{:S(2)}, u32[]{:S(2)}) collective-permute-start(f32[1,1,128,16]{2,3,1,0:T(8,128)S(1)} %bitcast.231), channel_id=1, source_target_pairs={{0,120},{8,128},{16,136},{24,144},{32,152},{40,160},{48,168},{56,1... | collective-permute-start | bytes 24584 | tf_op jit(solution)/shard_map/ppermute | solution.py:26
  114.3 20.9 %collective-permute-start.11 = (f32[1,1,128,16]{2,3,1,0:T(8,128)S(1)}, f32[1,1,128,16]{2,3,1,0:T(8,128)S(1)}, u32[]{:S(2)}, u32[]{:S(2)}) collective-permute-start(f32[1,1,128,16]{2,3,1,0:T(8,128)S(1)} %bitcast.230), channel_id=1, source_target_pairs={{0,112},{8,120},{16,128},{24,136},{32,144},{40,152},{48,160},{56,1... | collective-permute-start | bytes 24584 | tf_op jit(solution)/shard_map/ppermute | solution.py:26
  116.3 20.9 %collective-permute-start.12 = (f32[1,1,128,16]{2,3,1,0:T(8,128)S(1)}, f32[1,1,128,16]{2,3,1,0:T(8,128)S(1)}, u32[]{:S(2)}, u32[]{:S(2)}) collective-permute-start(f32[1,1,128,16]{2,3,1,0:T(8,128)S(1)} %bitcast.229), channel_id=1, source_target_pairs={{0,104},{8,112},{16,120},{24,128},{32,136},{40,144},{48,152},{56,1... | collective-permute-start | bytes 24584 | tf_op jit(solution)/shard_map/ppermute | solution.py:26
  118.2 20.9 %collective-permute-start.13 = (f32[1,1,128,16]{2,3,1,0:T(8,128)S(1)}, f32[1,1,128,16]{2,3,1,0:T(8,128)S(1)}, u32[]{:S(2)}, u32[]{:S(2)}) collective-permute-start(f32[1,1,128,16]{2,3,1,0:T(8,128)S(1)} %bitcast.228), channel_id=1, source_target_pairs={{0,96},{8,104},{16,112},{24,120},{32,128},{40,136},{48,144},{56,15... | collective-permute-start | bytes 24584 | tf_op jit(solution)/shard_map/ppermute | solution.py:26
  130.2 61.2 %collective-permute-start.14 = (f32[1,1,128,16]{2,3,1,0:T(8,128)}, f32[1,1,128,16]{2,3,1,0:T(8,128)S(1)}, u32[]{:S(2)}, u32[]{:S(2)}) collective-permute-start(f32[1,1,128,16]{2,3,1,0:T(8,128)} %bitcast.32), channel_id=1, source_target_pairs={{0,88},{8,96},{16,104},{24,112},{32,120},{40,128},{48,136},{56,144... | collective-permute-start | bytes 24584 | tf_op jit(solution)/shard_map/ppermute | solution.py:26
  133.3 60.1 %collective-permute-start.15 = (f32[1,1,128,16]{2,3,1,0:T(8,128)}, f32[1,1,128,16]{2,3,1,0:T(8,128)S(1)}, u32[]{:S(2)}, u32[]{:S(2)}) collective-permute-start(f32[1,1,128,16]{2,3,1,0:T(8,128)} %bitcast.34), channel_id=1, source_target_pairs={{0,80},{8,88},{16,96},{24,104},{32,112},{40,120},{48,128},{56,136}... | collective-permute-start | bytes 24584 | tf_op jit(solution)/shard_map/ppermute | solution.py:26
  135.2 60.1 %collective-permute-start.16 = (f32[1,1,128,16]{2,3,1,0:T(8,128)S(1)}, f32[1,1,128,16]{2,3,1,0:T(8,128)S(1)}, u32[]{:S(2)}, u32[]{:S(2)}) collective-permute-start(f32[1,1,128,16]{2,3,1,0:T(8,128)S(1)} %bitcast.245), channel_id=1, source_target_pairs={{0,72},{8,80},{16,88},{24,96},{32,104},{40,112},{48,120},{56,128},... | collective-permute-start | bytes 24584 | tf_op jit(solution)/shard_map/ppermute | solution.py:26
  137.2 60.1 %collective-permute-start.17 = (f32[1,1,128,16]{2,3,1,0:T(8,128)S(1)}, f32[1,1,128,16]{2,3,1,0:T(8,128)S(1)}, u32[]{:S(2)}, u32[]{:S(2)}) collective-permute-start(f32[1,1,128,16]{2,3,1,0:T(8,128)S(1)} %bitcast.239), channel_id=1, source_target_pairs={{0,64},{8,72},{16,80},{24,88},{32,96},{40,104},{48,112},{56,120},{... | collective-permute-start | bytes 24584 | tf_op jit(solution)/shard_map/ppermute | solution.py:26
  139.1 60.7 %collective-permute-start.18 = (f32[1,1,128,16]{2,3,1,0:T(8,128)S(1)}, f32[1,1,128,16]{2,3,1,0:T(8,128)S(1)}, u32[]{:S(2)}, u32[]{:S(2)}) collective-permute-start(f32[1,1,128,16]{2,3,1,0:T(8,128)S(1)} %bitcast.237), channel_id=1, source_target_pairs={{0,56},{8,64},{16,72},{24,80},{32,88},{40,96},{48,104},{56,112},{6... | collective-permute-start | bytes 24584 | tf_op jit(solution)/shard_map/ppermute | solution.py:26
  191.3 26.6 %collective-permute-start.19 = (f32[1,1,128,16]{2,3,1,0:T(8,128)}, f32[1,1,128,16]{2,3,1,0:T(8,128)}, u32[]{:S(2)}, u32[]{:S(2)}) collective-permute-start(f32[1,1,128,16]{2,3,1,0:T(8,128)} %bitcast.258), channel_id=1, source_target_pairs={{0,48},{8,56},{16,64},{24,72},{32,80},{40,88},{48,96},{56,104},{64... | collective-permute-start | bytes 24584 | tf_op jit(solution)/shard_map/ppermute | solution.py:26
  193.4 29.1 %collective-permute-start.20 = (f32[1,1,128,16]{2,3,1,0:T(8,128)}, f32[1,1,128,16]{2,3,1,0:T(8,128)}, u32[]{:S(2)}, u32[]{:S(2)}) collective-permute-start(f32[1,1,128,16]{2,3,1,0:T(8,128)} %bitcast.253), channel_id=1, source_target_pairs={{0,40},{8,48},{16,56},{24,64},{32,72},{40,80},{48,88},{56,96},{64,... | collective-permute-start | bytes 24584 | tf_op jit(solution)/shard_map/ppermute | solution.py:26
  195.4 35.7 %collective-permute-start.21 = (f32[1,1,128,16]{2,3,1,0:T(8,128)S(1)}, f32[1,1,128,16]{2,3,1,0:T(8,128)S(1)}, u32[]{:S(2)}, u32[]{:S(2)}) collective-permute-start(f32[1,1,128,16]{2,3,1,0:T(8,128)S(1)} %bitcast.247), channel_id=1, source_target_pairs={{0,32},{8,40},{16,48},{24,56},{32,64},{40,72},{48,80},{56,88},{64,... | collective-permute-start | bytes 24584 | tf_op jit(solution)/shard_map/ppermute | solution.py:26
  197.3 42.1 %collective-permute-start.22 = (f32[1,1,128,16]{2,3,1,0:T(8,128)S(1)}, f32[1,1,128,16]{2,3,1,0:T(8,128)S(1)}, u32[]{:S(2)}, u32[]{:S(2)}) collective-permute-start(f32[1,1,128,16]{2,3,1,0:T(8,128)S(1)} %bitcast.240), channel_id=1, source_target_pairs={{0,24},{8,32},{16,40},{24,48},{32,56},{40,64},{48,72},{56,80},{64,... | collective-permute-start | bytes 24584 | tf_op jit(solution)/shard_map/ppermute | solution.py:26
  199.8 48.8 %collective-permute-start.23 = (f32[1,1,128,16]{2,3,1,0:T(8,128)S(1)}, f32[1,1,128,16]{2,3,1,0:T(8,128)S(1)}, u32[]{:S(2)}, u32[]{:S(2)}) collective-permute-start(f32[1,1,128,16]{2,3,1,0:T(8,128)S(1)} %bitcast.236), channel_id=1, source_target_pairs={{0,16},{8,24},{16,32},{24,40},{32,48},{40,56},{48,64},{56,72},{64,... | collective-permute-start | bytes 24584 | tf_op jit(solution)/shard_map/ppermute | solution.py:26
  218.0 77.2 %collective-permute-start.24 = (f32[1,1,128,16]{2,3,1,0:T(8,128)S(1)}, f32[1,1,128,16]{2,3,1,0:T(8,128)S(1)}, u32[]{:S(2)}, u32[]{:S(2)}) collective-permute-start(f32[1,1,128,16]{2,3,1,0:T(8,128)S(1)} %bitcast.225), channel_id=1, source_target_pairs={{0,8},{8,16},{16,24},{24,32},{32,40},{40,48},{48,56},{56,64},{64,7... | collective-permute-start | bytes 24584 | tf_op jit(solution)/shard_map/ppermute | solution.py:26
  222.6 83.2 %collective-permute-start.26 = (f32[1,1,128,16]{2,3,1,0:T(8,128)S(1)}, f32[1,1,128,16]{2,3,1,0:T(8,128)S(1)}, u32[]{:S(2)}, u32[]{:S(2)}) collective-permute-start(f32[1,1,128,16]{2,3,1,0:T(8,128)S(1)} %bitcast.223), channel_id=1, source_target_pairs={{16,0},{24,8},{32,16},{40,24},{48,32},{56,40},{64,48},{72,56},{80,... | collective-permute-start | bytes 24584 | tf_op jit(solution)/shard_map/ppermute | solution.py:26
  231.1 86.1 %collective-permute-start.27 = (f32[1,1,128,16]{2,3,1,0:T(8,128)S(1)}, f32[1,1,128,16]{2,3,1,0:T(8,128)S(1)}, u32[]{:S(2)}, u32[]{:S(2)}) collective-permute-start(f32[1,1,128,16]{2,3,1,0:T(8,128)S(1)} %bitcast.222), channel_id=1, source_target_pairs={{24,0},{32,8},{40,16},{48,24},{56,32},{64,40},{72,48},{80,56},{88,... | collective-permute-start | bytes 24584 | tf_op jit(solution)/shard_map/ppermute | solution.py:26
  239.4 90.2 %collective-permute-start.28 = (f32[1,1,128,16]{2,3,1,0:T(8,128)S(1)}, f32[1,1,128,16]{2,3,1,0:T(8,128)S(1)}, u32[]{:S(2)}, u32[]{:S(2)}) collective-permute-start(f32[1,1,128,16]{2,3,1,0:T(8,128)S(1)} %bitcast.220), channel_id=1, source_target_pairs={{32,0},{40,8},{48,16},{56,24},{64,32},{72,40},{80,48},{88,56},{96,... | collective-permute-start | bytes 24584 | tf_op jit(solution)/shard_map/ppermute | solution.py:26
  248.6 91.3 %collective-permute-start.29 = (f32[1,1,128,16]{2,3,1,0:T(8,128)S(1)}, f32[1,1,128,16]{2,3,1,0:T(8,128)S(1)}, u32[]{:S(2)}, u32[]{:S(2)}) collective-permute-start(f32[1,1,128,16]{2,3,1,0:T(8,128)S(1)} %bitcast.219), channel_id=1, source_target_pairs={{40,0},{48,8},{56,16},{64,24},{72,32},{80,40},{88,48},{96,56},{104... | collective-permute-start | bytes 24584 | tf_op jit(solution)/shard_map/ppermute | solution.py:26
  295.2 48.5 %collective-permute-start.30 = (f32[1,1,128,16]{2,3,1,0:T(8,128)S(1)}, f32[1,1,128,16]{2,3,1,0:T(8,128)S(1)}, u32[]{:S(2)}, u32[]{:S(2)}) collective-permute-start(f32[1,1,128,16]{2,3,1,0:T(8,128)S(1)} %bitcast.218), channel_id=1, source_target_pairs={{48,0},{56,8},{64,16},{72,24},{80,32},{88,40},{96,48},{104,56},{11... | collective-permute-start | bytes 24584 | tf_op jit(solution)/shard_map/ppermute | solution.py:26
  305.7 39.9 %collective-permute-start.31 = (f32[1,1,128,16]{2,3,1,0:T(8,128)S(1)}, f32[1,1,128,16]{2,3,1,0:T(8,128)S(1)}, u32[]{:S(2)}, u32[]{:S(2)}) collective-permute-start(f32[1,1,128,16]{2,3,1,0:T(8,128)S(1)} %bitcast.217), channel_id=1, source_target_pairs={{56,0},{64,8},{72,16},{80,24},{88,32},{96,40},{104,48},{112,56},{1... | collective-permute-start | bytes 24584 | tf_op jit(solution)/shard_map/ppermute | solution.py:26
  317.2 30.4 %collective-permute-start.32 = (f32[1,1,128,16]{2,3,1,0:T(8,128)S(1)}, f32[1,1,128,16]{2,3,1,0:T(8,128)S(1)}, u32[]{:S(2)}, u32[]{:S(2)}) collective-permute-start(f32[1,1,128,16]{2,3,1,0:T(8,128)S(1)} %bitcast.216), channel_id=1, source_target_pairs={{64,0},{72,8},{80,16},{88,24},{96,32},{104,40},{112,48},{120,56},{... | collective-permute-start | bytes 24584 | tf_op jit(solution)/shard_map/ppermute | solution.py:26
  329.6 19.9 %collective-permute-start.33 = (f32[1,1,128,16]{2,3,1,0:T(8,128)S(1)}, f32[1,1,128,16]{2,3,1,0:T(8,128)S(1)}, u32[]{:S(2)}, u32[]{:S(2)}) collective-permute-start(f32[1,1,128,16]{2,3,1,0:T(8,128)S(1)} %bitcast.215), channel_id=1, source_target_pairs={{72,0},{80,8},{88,16},{96,24},{104,32},{112,40},{120,48},{128,56},... | collective-permute-start | bytes 24584 | tf_op jit(solution)/shard_map/ppermute | solution.py:26
  347.6 23.4 %collective-permute-start.37 = (f32[1,1,128,16]{2,3,1,0:T(8,128)S(1)}, f32[1,1,128,16]{2,3,1,0:T(8,128)S(1)}, u32[]{:S(2)}, u32[]{:S(2)}) collective-permute-start(f32[1,1,128,16]{2,3,1,0:T(8,128)S(1)} %bitcast.211), channel_id=1, source_target_pairs={{104,0},{112,8},{120,16},{128,24},{136,32},{144,40},{152,48},{160,... | collective-permute-start | bytes 24584 | tf_op jit(solution)/shard_map/ppermute | solution.py:26
  349.5 40.5 %collective-permute-start.38 = (f32[1,1,128,16]{2,3,1,0:T(8,128)S(1)}, f32[1,1,128,16]{2,3,1,0:T(8,128)S(1)}, u32[]{:S(2)}, u32[]{:S(2)}) collective-permute-start(f32[1,1,128,16]{2,3,1,0:T(8,128)S(1)} %bitcast.210), channel_id=1, source_target_pairs={{112,0},{120,8},{128,16},{136,24},{144,32},{152,40},{160,48},{168,... | collective-permute-start | bytes 24584 | tf_op jit(solution)/shard_map/ppermute | solution.py:26
  352.4 56.6 %collective-permute-start.39 = (f32[1,1,128,16]{2,3,1,0:T(8,128)S(1)}, f32[1,1,128,16]{2,3,1,0:T(8,128)S(1)}, u32[]{:S(2)}, u32[]{:S(2)}) collective-permute-start(f32[1,1,128,16]{2,3,1,0:T(8,128)S(1)} %bitcast.209), channel_id=1, source_target_pairs={{120,0},{128,8},{136,16},{144,24},{152,32},{160,40},{168,48},{176,... | collective-permute-start | bytes 24584 | tf_op jit(solution)/shard_map/ppermute | solution.py:26
  356.4 79.4 %collective-permute-start.40 = (f32[1,1,128,16]{2,3,1,0:T(8,128)S(1)}, f32[1,1,128,16]{2,3,1,0:T(8,128)S(1)}, u32[]{:S(2)}, u32[]{:S(2)}) collective-permute-start(f32[1,1,128,16]{2,3,1,0:T(8,128)S(1)} %bitcast.200), channel_id=1, source_target_pairs={{128,0},{136,8},{144,16},{152,24},{160,32},{168,40},{176,48},{184,... | collective-permute-start | bytes 24584 | tf_op jit(solution)/shard_map/ppermute | solution.py:26
  357.7 79.6 %collective-permute-start.41 = (f32[1,1,128,16]{2,3,1,0:T(8,128)S(1)}, f32[1,1,128,16]{2,3,1,0:T(8,128)S(1)}, u32[]{:S(2)}, u32[]{:S(2)}) collective-permute-start(f32[1,1,128,16]{2,3,1,0:T(8,128)S(1)} %bitcast.199), channel_id=1, source_target_pairs={{136,0},{144,8},{152,16},{160,24},{168,32},{176,40},{184,48},{192,... | collective-permute-start | bytes 24584 | tf_op jit(solution)/shard_map/ppermute | solution.py:26
  371.0 67.7 %collective-permute-start.42 = (f32[1,1,128,16]{2,3,1,0:T(8,128)S(1)}, f32[1,1,128,16]{2,3,1,0:T(8,128)S(1)}, u32[]{:S(2)}, u32[]{:S(2)}) collective-permute-start(f32[1,1,128,16]{2,3,1,0:T(8,128)S(1)} %bitcast.198), channel_id=1, source_target_pairs={{144,0},{152,8},{160,16},{168,24},{176,32},{184,40},{192,48},{200,... | collective-permute-start | bytes 24584 | tf_op jit(solution)/shard_map/ppermute | solution.py:26
  390.0 50.1 %collective-permute-start.43 = (f32[1,1,128,16]{2,3,1,0:T(8,128)S(1)}, f32[1,1,128,16]{2,3,1,0:T(8,128)S(1)}, u32[]{:S(2)}, u32[]{:S(2)}) collective-permute-start(f32[1,1,128,16]{2,3,1,0:T(8,128)S(1)} %bitcast.197), channel_id=1, source_target_pairs={{152,0},{160,8},{168,16},{176,24},{184,32},{192,40},{200,48},{208,... | collective-permute-start | bytes 24584 | tf_op jit(solution)/shard_map/ppermute | solution.py:26
  409.0 32.5 %collective-permute-start.25 = (f32[1,1,128,16]{2,3,1,0:T(8,128)S(1)}, f32[1,1,128,16]{2,3,1,0:T(8,128)S(1)}, u32[]{:S(2)}, u32[]{:S(2)}) collective-permute-start(f32[1,1,128,16]{2,3,1,0:T(8,128)S(1)} %bitcast.265), channel_id=1, source_target_pairs={{8,0},{16,8},{24,16},{32,24},{40,32},{48,40},{56,48},{64,56},{72,6... | collective-permute-start | bytes 24584 | tf_op jit(solution)/shard_map/ppermute | solution.py:26
  573.6 19.3 %collective-permute-start.50 = (f32[1,1,128,16]{2,3,1,0:T(8,128)S(1)}, f32[1,1,128,16]{2,3,1,0:T(8,128)S(1)}, u32[]{:S(2)}, u32[]{:S(2)}) collective-permute-start(f32[1,1,128,16]{2,3,1,0:T(8,128)S(1)} %bitcast.331), channel_id=1, source_target_pairs={{0,128},{8,136},{16,144},{24,152},{32,160},{40,168},{48,176},{56,1... | collective-permute-start | bytes 24584 | tf_op jit(solution)/shard_map/ppermute | solution.py:26
  576.6 26.4 %collective-permute-start.51 = (f32[1,1,128,16]{2,3,1,0:T(8,128)S(1)}, f32[1,1,128,16]{2,3,1,0:T(8,128)S(1)}, u32[]{:S(2)}, u32[]{:S(2)}) collective-permute-start(f32[1,1,128,16]{2,3,1,0:T(8,128)S(1)} %bitcast.327), channel_id=1, source_target_pairs={{0,120},{8,128},{16,136},{24,144},{32,152},{40,160},{48,168},{56,1... | collective-permute-start | bytes 24584 | tf_op jit(solution)/shard_map/ppermute | solution.py:26
  581.1 23.9 %collective-permute-start.52 = (f32[1,1,128,16]{2,3,1,0:T(8,128)S(1)}, f32[1,1,128,16]{2,3,1,0:T(8,128)S(1)}, u32[]{:S(2)}, u32[]{:S(2)}) collective-permute-start(f32[1,1,128,16]{2,3,1,0:T(8,128)S(1)} %bitcast.325), channel_id=1, source_target_pairs={{0,112},{8,120},{16,128},{24,136},{32,144},{40,152},{48,160},{56,1... | collective-permute-start | bytes 24584 | tf_op jit(solution)/shard_map/ppermute | solution.py:26
  584.6 22.3 %collective-permute-start.53 = (f32[1,1,128,16]{2,3,1,0:T(8,128)S(1)}, f32[1,1,128,16]{2,3,1,0:T(8,128)S(1)}, u32[]{:S(2)}, u32[]{:S(2)}) collective-permute-start(f32[1,1,128,16]{2,3,1,0:T(8,128)S(1)} %bitcast.323), channel_id=1, source_target_pairs={{0,104},{8,112},{16,120},{24,128},{32,136},{40,144},{48,152},{56,1... | collective-permute-start | bytes 24584 | tf_op jit(solution)/shard_map/ppermute | solution.py:26
  588.2 20.6 %collective-permute-start.54 = (f32[1,1,128,16]{2,3,1,0:T(8,128)S(1)}, f32[1,1,128,16]{2,3,1,0:T(8,128)S(1)}, u32[]{:S(2)}, u32[]{:S(2)}) collective-permute-start(f32[1,1,128,16]{2,3,1,0:T(8,128)S(1)} %bitcast.321), channel_id=1, source_target_pairs={{0,96},{8,104},{16,112},{24,120},{32,128},{40,136},{48,144},{56,15... | collective-permute-start | bytes 24584 | tf_op jit(solution)/shard_map/ppermute | solution.py:26
  592.9 20.3 %collective-permute-start.55 = (f32[1,1,128,16]{2,3,1,0:T(8,128)S(1)}, f32[1,1,128,16]{2,3,1,0:T(8,128)S(1)}, u32[]{:S(2)}, u32[]{:S(2)}) collective-permute-start(f32[1,1,128,16]{2,3,1,0:T(8,128)S(1)} %bitcast.318), channel_id=1, source_target_pairs={{0,88},{8,96},{16,104},{24,112},{32,120},{40,128},{48,136},{56,144... | collective-permute-start | bytes 24584 | tf_op jit(solution)/shard_map/ppermute | solution.py:26
  603.0 18.4 %collective-permute-start.56 = (f32[1,1,128,16]{2,3,1,0:T(8,128)S(1)}, f32[1,1,128,16]{2,3,1,0:T(8,128)S(1)}, u32[]{:S(2)}, u32[]{:S(2)}) collective-permute-start(f32[1,1,128,16]{2,3,1,0:T(8,128)S(1)} %bitcast.308), channel_id=1, source_target_pairs={{0,80},{8,88},{16,96},{24,104},{32,112},{40,120},{48,128},{56,136}... | collective-permute-start | bytes 24584 | tf_op jit(solution)/shard_map/ppermute | solution.py:26
  604.9 18.4 %collective-permute-start.57 = (f32[1,1,128,16]{2,3,1,0:T(8,128)S(1)}, f32[1,1,128,16]{2,3,1,0:T(8,128)S(1)}, u32[]{:S(2)}, u32[]{:S(2)}) collective-permute-start(f32[1,1,128,16]{2,3,1,0:T(8,128)S(1)} %bitcast.301), channel_id=1, source_target_pairs={{0,72},{8,80},{16,88},{24,96},{32,104},{40,112},{48,120},{56,128},... | collective-permute-start | bytes 24584 | tf_op jit(solution)/shard_map/ppermute | solution.py:26
  606.9 18.8 %collective-permute-start.58 = (f32[1,1,128,16]{2,3,1,0:T(8,128)S(1)}, f32[1,1,128,16]{2,3,1,0:T(8,128)S(1)}, u32[]{:S(2)}, u32[]{:S(2)}) collective-permute-start(f32[1,1,128,16]{2,3,1,0:T(8,128)S(1)} %bitcast.293), channel_id=1, source_target_pairs={{0,64},{8,72},{16,80},{24,88},{32,96},{40,104},{48,112},{56,120},{... | collective-permute-start | bytes 24584 | tf_op jit(solution)/shard_map/ppermute | solution.py:26
  608.8 19.0 %collective-permute-start.59 = (f32[1,1,128,16]{2,3,1,0:T(8,128)S(1)}, f32[1,1,128,16]{2,3,1,0:T(8,128)S(1)}, u32[]{:S(2)}, u32[]{:S(2)}) collective-permute-start(f32[1,1,128,16]{2,3,1,0:T(8,128)S(1)} %bitcast.286), channel_id=1, source_target_pairs={{0,56},{8,64},{16,72},{24,80},{32,88},{40,96},{48,104},{56,112},{6... | collective-permute-start | bytes 24584 | tf_op jit(solution)/shard_map/ppermute | solution.py:26
  621.5 24.4 %collective-permute-start.61 = (f32[1,1,128,16]{2,3,1,0:T(8,128)S(1)}, f32[1,1,128,16]{2,3,1,0:T(8,128)S(1)}, u32[]{:S(2)}, u32[]{:S(2)}) collective-permute-start(f32[1,1,128,16]{2,3,1,0:T(8,128)S(1)} %bitcast.295), channel_id=1, source_target_pairs={{0,40},{8,48},{16,56},{24,64},{32,72},{40,80},{48,88},{56,96},{64,... | collective-permute-start | bytes 24584 | tf_op jit(solution)/shard_map/ppermute | solution.py:26
  623.4 23.9 %collective-permute-start.62 = (f32[1,1,128,16]{2,3,1,0:T(8,128)S(1)}, f32[1,1,128,16]{2,3,1,0:T(8,128)S(1)}, u32[]{:S(2)}, u32[]{:S(2)}) collective-permute-start(f32[1,1,128,16]{2,3,1,0:T(8,128)S(1)} %bitcast.288), channel_id=1, source_target_pairs={{0,32},{8,40},{16,48},{24,56},{32,64},{40,72},{48,80},{56,88},{64,... | collective-permute-start | bytes 24584 | tf_op jit(solution)/shard_map/ppermute | solution.py:26
  625.7 23.0 %collective-permute-start.63 = (f32[1,1,128,16]{2,3,1,0:T(8,128)S(1)}, f32[1,1,128,16]{2,3,1,0:T(8,128)S(1)}, u32[]{:S(2)}, u32[]{:S(2)}) collective-permute-start(f32[1,1,128,16]{2,3,1,0:T(8,128)S(1)} %bitcast.283), channel_id=1, source_target_pairs={{0,24},{8,32},{16,40},{24,48},{32,56},{40,64},{48,72},{56,80},{64,... | collective-permute-start | bytes 24584 | tf_op jit(solution)/shard_map/ppermute | solution.py:26
  627.8 22.4 %collective-permute-start.64 = (f32[1,1,128,16]{2,3,1,0:T(8,128)S(1)}, f32[1,1,128,16]{2,3,1,0:T(8,128)S(1)}, u32[]{:S(2)}, u32[]{:S(2)}) collective-permute-start(f32[1,1,128,16]{2,3,1,0:T(8,128)S(1)} %bitcast.279), channel_id=1, source_target_pairs={{0,16},{8,24},{16,32},{24,40},{32,48},{40,56},{48,64},{56,72},{64,... | collective-permute-start | bytes 24584 | tf_op jit(solution)/shard_map/ppermute | solution.py:26
  629.8 21.8 %collective-permute-start.65 = (f32[1,1,128,16]{2,3,1,0:T(8,128)S(1)}, f32[1,1,128,16]{2,3,1,0:T(8,128)S(1)}, u32[]{:S(2)}, u32[]{:S(2)}) collective-permute-start(f32[1,1,128,16]{2,3,1,0:T(8,128)S(1)} %bitcast.273), channel_id=1, source_target_pairs={{0,8},{8,16},{16,24},{24,32},{32,40},{40,48},{48,56},{56,64},{64,7... | collective-permute-start | bytes 24584 | tf_op jit(solution)/shard_map/ppermute | solution.py:26
  694.4 41.4 %collective-permute-start.66 = (f32[1,1,128,16]{2,3,1,0:T(8,128)S(1)}, f32[1,1,128,16]{2,3,1,0:T(8,128)S(1)}, u32[]{:S(2)}, u32[]{:S(2)}) collective-permute-start(f32[1,1,128,16]{2,3,1,0:T(8,128)S(1)} %bitcast.332), channel_id=1, source_target_pairs={{8,0},{16,8},{24,16},{32,24},{40,32},{48,40},{56,48},{64,56},{72,6... | collective-permute-start | bytes 24584 | tf_op jit(solution)/shard_map/ppermute | solution.py:26
  701.5 54.4 %collective-permute-start.67 = (f32[1,1,128,16]{2,3,1,0:T(8,128)S(1)}, f32[1,1,128,16]{2,3,1,0:T(8,128)S(1)}, u32[]{:S(2)}, u32[]{:S(2)}) collective-permute-start(f32[1,1,128,16]{2,3,1,0:T(8,128)S(1)} %bitcast.328), channel_id=1, source_target_pairs={{16,0},{24,8},{32,16},{40,24},{48,32},{56,40},{64,48},{72,56},{80,... | collective-permute-start | bytes 24584 | tf_op jit(solution)/shard_map/ppermute | solution.py:26
  707.9 57.7 %collective-permute-start.68 = (f32[1,1,128,16]{2,3,1,0:T(8,128)S(1)}, f32[1,1,128,16]{2,3,1,0:T(8,128)S(1)}, u32[]{:S(2)}, u32[]{:S(2)}) collective-permute-start(f32[1,1,128,16]{2,3,1,0:T(8,128)S(1)} %bitcast.326), channel_id=1, source_target_pairs={{24,0},{32,8},{40,16},{48,24},{56,32},{64,40},{72,48},{80,56},{88,... | collective-permute-start | bytes 24584 | tf_op jit(solution)/shard_map/ppermute | solution.py:26
  716.4 61.6 %collective-permute-start.69 = (f32[1,1,128,16]{2,3,1,0:T(8,128)S(1)}, f32[1,1,128,16]{2,3,1,0:T(8,128)S(1)}, u32[]{:S(2)}, u32[]{:S(2)}) collective-permute-start(f32[1,1,128,16]{2,3,1,0:T(8,128)S(1)} %bitcast.324), channel_id=1, source_target_pairs={{32,0},{40,8},{48,16},{56,24},{64,32},{72,40},{80,48},{88,56},{96,... | collective-permute-start | bytes 24584 | tf_op jit(solution)/shard_map/ppermute | solution.py:26
  725.4 62.7 %collective-permute-start.70 = (f32[1,1,128,16]{2,3,1,0:T(8,128)S(1)}, f32[1,1,128,16]{2,3,1,0:T(8,128)S(1)}, u32[]{:S(2)}, u32[]{:S(2)}) collective-permute-start(f32[1,1,128,16]{2,3,1,0:T(8,128)S(1)} %bitcast.322), channel_id=1, source_target_pairs={{40,0},{48,8},{56,16},{64,24},{72,32},{80,40},{88,48},{96,56},{104... | collective-permute-start | bytes 24584 | tf_op jit(solution)/shard_map/ppermute | solution.py:26
  735.8 54.4 %collective-permute-start.71 = (f32[1,1,128,16]{2,3,1,0:T(8,128)S(1)}, f32[1,1,128,16]{2,3,1,0:T(8,128)S(1)}, u32[]{:S(2)}, u32[]{:S(2)}) collective-permute-start(f32[1,1,128,16]{2,3,1,0:T(8,128)S(1)} %bitcast.320), channel_id=1, source_target_pairs={{48,0},{56,8},{64,16},{72,24},{80,32},{88,40},{96,48},{104,56},{11... | collective-permute-start | bytes 24584 | tf_op jit(solution)/shard_map/ppermute | solution.py:26
  755.9 42.0 %collective-permute-start.72 = (f32[1,1,128,16]{2,3,1,0:T(8,128)S(1)}, f32[1,1,128,16]{2,3,1,0:T(8,128)S(1)}, u32[]{:S(2)}, u32[]{:S(2)}) collective-permute-start(f32[1,1,128,16]{2,3,1,0:T(8,128)S(1)} %bitcast.311), channel_id=1, source_target_pairs={{56,0},{64,8},{72,16},{80,24},{88,32},{96,40},{104,48},{112,56},{1... | collective-permute-start | bytes 24584 | tf_op jit(solution)/shard_map/ppermute | solution.py:26
  765.6 34.2 %collective-permute-start.73 = (f32[1,1,128,16]{2,3,1,0:T(8,128)S(1)}, f32[1,1,128,16]{2,3,1,0:T(8,128)S(1)}, u32[]{:S(2)}, u32[]{:S(2)}) collective-permute-start(f32[1,1,128,16]{2,3,1,0:T(8,128)S(1)} %bitcast.304), channel_id=1, source_target_pairs={{64,0},{72,8},{80,16},{88,24},{96,32},{104,40},{112,48},{120,56},{... | collective-permute-start | bytes 24584 | tf_op jit(solution)/shard_map/ppermute | solution.py:26
  778.0 23.8 %collective-permute-start.74 = (f32[1,1,128,16]{2,3,1,0:T(8,128)S(1)}, f32[1,1,128,16]{2,3,1,0:T(8,128)S(1)}, u32[]{:S(2)}, u32[]{:S(2)}) collective-permute-start(f32[1,1,128,16]{2,3,1,0:T(8,128)S(1)} %bitcast.299), channel_id=1, source_target_pairs={{72,0},{80,8},{88,16},{96,24},{104,32},{112,40},{120,48},{128,56},... | collective-permute-start | bytes 24584 | tf_op jit(solution)/shard_map/ppermute | solution.py:26
  797.9 22.0 %collective-permute-start.77 = (f32[1,1,128,16]{2,3,1,0:T(8,128)S(1)}, f32[1,1,128,16]{2,3,1,0:T(8,128)S(1)}, u32[]{:S(2)}, u32[]{:S(2)}) collective-permute-start(f32[1,1,128,16]{2,3,1,0:T(8,128)S(1)} %bitcast.291), channel_id=1, source_target_pairs={{96,0},{104,8},{112,16},{120,24},{128,32},{136,40},{144,48},{152,5... | collective-permute-start | bytes 24584 | tf_op jit(solution)/shard_map/ppermute | solution.py:26
  799.9 21.5 %collective-permute-start.78 = (f32[1,1,128,16]{2,3,1,0:T(8,128)S(1)}, f32[1,1,128,16]{2,3,1,0:T(8,128)S(1)}, u32[]{:S(2)}, u32[]{:S(2)}) collective-permute-start(f32[1,1,128,16]{2,3,1,0:T(8,128)S(1)} %bitcast.284), channel_id=1, source_target_pairs={{104,0},{112,8},{120,16},{128,24},{136,32},{144,40},{152,48},{160,... | collective-permute-start | bytes 24584 | tf_op jit(solution)/shard_map/ppermute | solution.py:26
  801.8 21.0 %collective-permute-start.79 = (f32[1,1,128,16]{2,3,1,0:T(8,128)S(1)}, f32[1,1,128,16]{2,3,1,0:T(8,128)S(1)}, u32[]{:S(2)}, u32[]{:S(2)}) collective-permute-start(f32[1,1,128,16]{2,3,1,0:T(8,128)S(1)} %bitcast.280), channel_id=1, source_target_pairs={{112,0},{120,8},{128,16},{136,24},{144,32},{152,40},{160,48},{168,... | collective-permute-start | bytes 24584 | tf_op jit(solution)/shard_map/ppermute | solution.py:26
  803.7 20.5 %collective-permute-start.80 = (f32[1,1,128,16]{2,3,1,0:T(8,128)S(1)}, f32[1,1,128,16]{2,3,1,0:T(8,128)S(1)}, u32[]{:S(2)}, u32[]{:S(2)}) collective-permute-start(f32[1,1,128,16]{2,3,1,0:T(8,128)S(1)} %bitcast.275), channel_id=1, source_target_pairs={{120,0},{128,8},{136,16},{144,24},{152,32},{160,40},{168,48},{176,... | collective-permute-start | bytes 24584 | tf_op jit(solution)/shard_map/ppermute | solution.py:26
  805.7 19.9 %collective-permute-start.81 = (f32[1,1,128,16]{2,3,1,0:T(8,128)S(1)}, f32[1,1,128,16]{2,3,1,0:T(8,128)S(1)}, u32[]{:S(2)}, u32[]{:S(2)}) collective-permute-start(f32[1,1,128,16]{2,3,1,0:T(8,128)S(1)} %bitcast.270), channel_id=1, source_target_pairs={{128,0},{136,8},{144,16},{152,24},{160,32},{168,40},{176,48},{184,... | collective-permute-start | bytes 24584 | tf_op jit(solution)/shard_map/ppermute | solution.py:26
  (21 other events, 350.7 us)
where the time goes:
time: 895 us; the launch traced here: 880 us
  local copies, waits for them, and re-layouts  449 us (50%)
  starting transfers between devices  380 us (42%)
  waiting for transfers between devices  20.2 us (2%)
  other arithmetic  14.6 us (2%)
  blocking collectives  14.6 us (2%)
    ppermute x70, starting transfers between devices, from_behind(): return lax.ppermute(shard, axis, pairs)  358 us
    unnamed x77, local copies, waits for them, and re-layouts  144 us
    dynamic_slice x76, local copies, waits for them, and re-layouts, piece_for(): return lax.dynamic_index_in_dim(tile_blocks, target, axis=1, keepdims=False)  142 us
    another operation x74, local copies, waits for them, and re-layouts, relayout(): window = jnp.stack(received[::-1], axis=0)  136 us
    dynamic_update_slice x2, local copies, waits for them, and re-layouts, relayout(): padded = lax.dynamic_update_slice_in_dim(padded, window, device_index, 0)  21.2 us
  transfers between devices with their start and end apart: 83, of which 8 were waited for; matrix products, arithmetic and copies ran while one was open for 28% of the time, Pallas kernels for 0%

commit v1 on v0

--- a/solution.py
+++ b/solution.py
@@ -4,6 +4,18 @@
 from jax.sharding import PartitionSpec as P
 
 STEPS = 3
+
+
+def split_up(value, dim, size):
+    lengths = value.shape
+    blocks = value.reshape(*lengths[:dim], size, lengths[dim] // size, *lengths[dim + 1 :])
+    return jnp.moveaxis(blocks, dim, 0)
+
+
+def in_order(blocks, dim):
+    blocks = jnp.moveaxis(blocks, 0, dim)
+    lengths = blocks.shape
+    return blocks.reshape(*lengths[:dim], lengths[dim] * lengths[dim + 1], *lengths[dim + 2 :])
 
 
 def extended_2(block, sides, width):
@@ -55,7 +67,14 @@
 def relayout(block, reach_rows):
     row_count = block.shape[0]
     lat_count = block.shape[1]
-    swapped = lax.all_to_all(block, "lon", split_axis=3, concat_axis=2, tiled=True)
+    peers, index = (lax.axis_size("lon"), lax.axis_index("lon"))
+    blocks = split_up(block, 3, peers)
+    finished = [blocks[index]]
+    for step in range(1, peers):
+        sent = blocks[index ^ step]
+        finished.append(lax.ppermute(sent, "lon", [(i_2, i_2 ^ step) for i_2 in range(peers)]))
+    blocks = jnp.stack(finished)[index ^ jnp.arange(peers)]
+    swapped = in_order(blocks, 2)
     lon_count = swapped.shape[2]
     col_count = swapped.shape[3]
     block_count = lat_count // row_count

time: 895 us -> 1000 us (1.12)
  starting transfers between devices: 380 us -> 584 us
  local copies, waits for them, and re-layouts: 449 us -> 371 us
  blocking collectives: 14.6 us -> 0 us
    ppermute x0 -> x14, starting transfers between devices: none -> 203 us  [relayout(): lax.ppermute(sent, 'lon', [(i_2, i_2 ^ step) for i_2 in range(peers)])]
    unnamed x77 -> x55, local copies, waits for them, and re-layouts: 144 us -> 76.8 us
    all_to_all x1 -> x0, blocking collectives: 14.6 us -> none  [relayout(): lax.all_to_all(block, 'lon', split_axis=3, concat_axis=2, tiled=True)]
    dynamic_update_slice x2, local copies, waits for them, and re-layouts: 21.2 us -> 7.18 us  [relayout(): padded = lax.dynamic_update_slice_in_dim(padded, window, device_index, 0)]
    ppermute x0 -> x14, waiting for transfers between devices: none -> 11.8 us  [relayout(): lax.ppermute(sent, 'lon', [(i_2, i_2 ^ step) for i_2 in range(peers)])]
    all_to_all x1 -> x0, waiting for transfers between devices: 10.3 us -> none  [relayout(): lax.all_to_all(block, 'lon', split_axis=3, concat_axis=2, tiled=True)]
    dynamic_slice x76 -> x75, local copies, waits for them, and re-layouts: 142 us -> 143 us  [piece_for(): return lax.dynamic_index_in_dim(tile_blocks, target, axis=1, keepdims=False)]
    another operation x74 -> x73, local copies, waits for them, and re-layouts: 136 us -> 138 us  [relayout(): window = jnp.stack(received[::-1], axis=0)]
  transfers between devices with their start and end apart: 83 -> 96, of which waited for: 8 -> 8; matrix products, arithmetic and copies ran while one was open for 28% -> 22% of each run, Pallas kernels for 0% -> 0%
where the time goes in v1:
time: 1000 us; the launch traced here: 988 us
  starting transfers between devices  584 us (58%)
  local copies, waits for them, and re-layouts  371 us (37%)
  waiting for transfers between devices  20.5 us (2%)
  other arithmetic  10.2 us (1%)
    ppermute x70, starting transfers between devices, from_behind(): return lax.ppermute(shard, axis, pairs)  363 us
    ppermute x14, starting transfers between devices, relayout(): lax.ppermute(sent, 'lon', [(i_2, i_2 ^ step) for i_2 in range(peers)])  203 us
    dynamic_slice x75, local copies, waits for them, and re-layouts, piece_for(): return lax.dynamic_index_in_dim(tile_blocks, target, axis=1, keepdims=False)  143 us
    another operation x73, local copies, waits for them, and re-layouts, relayout(): window = jnp.stack(received[::-1], axis=0)  138 us
    unnamed x55, local copies, waits for them, and re-layouts  76.8 us
  transfers between devices with their start and end apart: 96, of which 8 were waited for; matrix products, arithmetic and copies ran while one was open for 22% of the time, Pallas kernels for 0%

profile of v1, /device:TPU:24, one launch (start us, length us, event | category | flops | bytes accessed | tf_op | source)
XLA Modules:
  0.0 987.6 jit_solution(14506343784714071860)
XLA Ops:
  2.2 2.9 collective-permute-start.1
  9.1 2.6 collective-permute-start.3
  15.3 3.0 collective-permute-start.5
  25.7 22.2 %collective-permute-start.8 = (f32[1,64,16,16]{1,3,2,0:T(8,128)S(1)}, f32[1,64,16,16]{1,3,2,0:T(8,128)S(1)}, u32[]{:S(2)}, u32[]{:S(2)}) collective-permute-start(f32[1,64,16,16]{1,3,2,0:T(8,128)S(1)} %get-tuple-element.100), channel_id=1, source_target_pairs={{0,3},{1,2},{2,1},{3,0},{4,7},{5,6},{6,5},{7,4},{8,11},{9,10},{10,... | collective-permute-start | bytes 196616 | tf_op jit(solution)/shard_map/ppermute | solution.py:75
  48.0 19.0 %collective-permute-start.9 = (f32[1,64,16,16]{1,3,2,0:T(8,128)S(1)}, f32[1,64,16,16]{1,3,2,0:T(8,128)S(1)}, u32[]{:S(2)}, u32[]{:S(2)}) collective-permute-start(f32[1,64,16,16]{1,3,2,0:T(8,128)S(1)} %get-tuple-element.99), channel_id=1, source_target_pairs={{0,4},{1,5},{2,6},{3,7},{4,0},{5,1},{6,2},{7,3},{8,12},{9,13},{10,... | collective-permute-start | bytes 196616 | tf_op jit(solution)/shard_map/ppermute | solution.py:75
  67.0 19.0 %collective-permute-start.10 = (f32[1,64,16,16]{1,3,2,0:T(8,128)S(1)}, f32[1,64,16,16]{1,3,2,0:T(8,128)S(1)}, u32[]{:S(2)}, u32[]{:S(2)}) collective-permute-start(f32[1,64,16,16]{1,3,2,0:T(8,128)S(1)} %get-tuple-element.98), channel_id=1, source_target_pairs={{0,5},{1,4},{2,7},{3,6},{4,1},{5,0},{6,3},{7,2},{8,13},{9,12},{10,... | collective-permute-start | bytes 196616 | tf_op jit(solution)/shard_map/ppermute | solution.py:75
  86.0 19.0 %collective-permute-start.11 = (f32[1,64,16,16]{1,3,2,0:T(8,128)S(1)}, f32[1,64,16,16]{1,3,2,0:T(8,128)S(1)}, u32[]{:S(2)}, u32[]{:S(2)}) collective-permute-start(f32[1,64,16,16]{1,3,2,0:T(8,128)S(1)} %get-tuple-element.97), channel_id=1, source_target_pairs={{0,6},{1,7},{2,4},{3,5},{4,2},{5,3},{6,0},{7,1},{8,14},{9,15},{10,... | collective-permute-start | bytes 196616 | tf_op jit(solution)/shard_map/ppermute | solution.py:75
  105.1 19.0 %collective-permute-start.12 = (f32[1,64,16,16]{1,3,2,0:T(8,128)S(1)}, f32[1,64,16,16]{1,3,2,0:T(8,128)S(1)}, u32[]{:S(2)}, u32[]{:S(2)}) collective-permute-start(f32[1,64,16,16]{1,3,2,0:T(8,128)S(1)} %get-tuple-element.96), channel_id=1, source_target_pairs={{0,7},{1,6},{2,5},{3,4},{4,3},{5,2},{6,1},{7,0},{8,15},{9,14},{10,... | collective-permute-start | bytes 196616 | tf_op jit(solution)/shard_map/ppermute | solution.py:75
  124.2 5.9 collective-permute-done.12
  130.8 8.4 constant_dynamic-slice_fusion.32
  140.8 9.5 collective-permute-start.33
  151.9 5.6 collective-permute-start.34
  159.1 4.1 collective-permute-start.35
  168.4 9.1 collective-permute-start.37
  182.4 5.6 collective-permute-start.38
  188.1 8.2 collective-permute-start.39
  196.3 4.3 collective-permute-start.40
  227.5 11.2 %collective-permute-start.48 = (f32[1,1,128,16]{2,3,1,0:T(8,128)S(1)}, f32[1,1,128,16]{2,3,1,0:T(8,128)S(1)}, u32[]{:S(2)}, u32[]{:S(2)}) collective-permute-start(f32[1,1,128,16]{2,3,1,0:T(8,128)S(1)} %bitcast.325), channel_id=1, source_target_pairs={{136,0},{144,8},{152,16},{160,24},{168,32},{176,40},{184,48},{192,... | collective-permute-start | bytes 24584 | tf_op jit(solution)/shard_map/ppermute | solution.py:38
  238.8 19.0 %collective-permute-start.49 = (f32[1,1,128,16]{2,3,1,0:T(8,128)S(1)}, f32[1,1,128,16]{2,3,1,0:T(8,128)S(1)}, u32[]{:S(2)}, u32[]{:S(2)}) collective-permute-start(f32[1,1,128,16]{2,3,1,0:T(8,128)S(1)} %bitcast.319), channel_id=1, source_target_pairs={{144,0},{152,8},{160,16},{168,24},{176,32},{184,40},{192,48},{200,... | collective-permute-start | bytes 24584 | tf_op jit(solution)/shard_map/ppermute | solution.py:38
  257.8 19.0 %collective-permute-start.50 = (f32[1,1,128,16]{2,3,1,0:T(8,128)S(1)}, f32[1,1,128,16]{2,3,1,0:T(8,128)S(1)}, u32[]{:S(2)}, u32[]{:S(2)}) collective-permute-start(f32[1,1,128,16]{2,3,1,0:T(8,128)S(1)} %bitcast.316), channel_id=1, source_target_pairs={{152,0},{160,8},{168,16},{176,24},{184,32},{192,40},{200,48},{208,... | collective-permute-start | bytes 24584 | tf_op jit(solution)/shard_map/ppermute | solution.py:38
  276.9 8.4 constant_dynamic-slice_fusion.50
  294.7 8.6 collective-permute-start.17
  317.3 3.1 collective-permute-start.21
  326.3 4.8 collective-permute-start.25
  348.6 2.5 collective-permute-start.29
  353.0 2.6 constant_dynamic-slice_fusion.68
  362.5 2.5 collective-permute-start.31
  365.0 5.5 collective-permute-start.32
  370.5 35.0 %collective-permute-start.13 = (f32[1,1,128,16]{2,3,1,0:T(8,128)S(1)}, f32[1,1,128,16]{2,3,1,0:T(8,128)}, u32[]{:S(2)}, u32[]{:S(2)}) collective-permute-start(f32[1,1,128,16]{2,3,1,0:T(8,128)S(1)} %bitcast.303), channel_id=1, source_target_pairs={{0,152},{8,160},{16,168},{24,176},{32,184},{40,192},{48,200},{56,2... | collective-permute-start | bytes 24584 | tf_op jit(solution)/shard_map/ppermute | solution.py:38
  405.5 19.0 %collective-permute-start.14 = (f32[1,1,128,16]{2,3,1,0:T(8,128)S(1)}, f32[1,1,128,16]{2,3,1,0:T(8,128)}, u32[]{:S(2)}, u32[]{:S(2)}) collective-permute-start(f32[1,1,128,16]{2,3,1,0:T(8,128)S(1)} %bitcast.299), channel_id=1, source_target_pairs={{0,144},{8,152},{16,160},{24,168},{32,176},{40,184},{48,192},{56,2... | collective-permute-start | bytes 24584 | tf_op jit(solution)/shard_map/ppermute | solution.py:38
  424.5 19.0 %collective-permute-start.15 = (f32[1,1,128,16]{2,3,1,0:T(8,128)S(1)}, f32[1,1,128,16]{2,3,1,0:T(8,128)}, u32[]{:S(2)}, u32[]{:S(2)}) collective-permute-start(f32[1,1,128,16]{2,3,1,0:T(8,128)S(1)} %bitcast.297), channel_id=1, source_target_pairs={{0,136},{8,144},{16,152},{24,160},{32,168},{40,176},{48,184},{56,1... | collective-permute-start | bytes 24584 | tf_op jit(solution)/shard_map/ppermute | solution.py:38
  444.6 12.1 %copy.525 = f32[1,1,1,128,16]{0,3,4,2,1:T(8,128)S(1)} copy(f32[1,1,1,128,16]{1,4,3,2,0:T(8,128)S(1)} %get-tuple-element.76) | data formatting | bytes 16384
  509.8 23.2 %stack.312 = f32[39,1,1,128,16]{0,3,4,2,1:T(8,128)} concatenate(f32[1,1,1,128,16]{0,3,4,2,1:T(8,128)} %copy.422, f32[1,1,1,128,16]{0,3,4,2,1:T(8,128)} %copy.423, f32[1,1,1,128,16]{0,3,4,2,1:T(8,128)} %copy.424, f32[1,1,1,128,16]{0,3,4,2,1:T(8,128)} %copy.425, f32[1,1,1,128,16]{0,3,4,2,1:T(8,128)} %copy.426, f32[1,1,1,128,16]{0,3,4,2,1:T(8,128)} %copy.427, ...), dimensions={0} | concatenate | bytes 638976 | tf_op jit(solution)/shard_map/stack | solution.py:96
  533.1 7.2 dynamic_update_slice.6
  540.8 2.8 collective-permute-start.52
  546.9 2.6 collective-permute-start.54
  552.4 3.0 collective-permute-start.56
  562.2 21.5 %collective-permute-start.59 = (f32[1,64,16,16]{1,3,2,0:T(8,128)S(1)}, f32[1,64,16,16]{1,3,2,0:T(8,128)S(1)}, u32[]{:S(2)}, u32[]{:S(2)}) collective-permute-start(f32[1,64,16,16]{1,3,2,0:T(8,128)S(1)} %get-tuple-element.42), channel_id=1, source_target_pairs={{0,3},{1,2},{2,1},{3,0},{4,7},{5,6},{6,5},{7,4},{8,11},{9,10},{10,... | collective-permute-start | bytes 196616 | tf_op jit(solution)/shard_map/ppermute | solution.py:75
  583.6 19.0 %collective-permute-start.60 = (f32[1,64,16,16]{1,3,2,0:T(8,128)S(1)}, f32[1,64,16,16]{1,3,2,0:T(8,128)S(1)}, u32[]{:S(2)}, u32[]{:S(2)}) collective-permute-start(f32[1,64,16,16]{1,3,2,0:T(8,128)S(1)} %get-tuple-element.41), channel_id=1, source_target_pairs={{0,4},{1,5},{2,6},{3,7},{4,0},{5,1},{6,2},{7,3},{8,12},{9,13},{10,... | collective-permute-start | bytes 196616 | tf_op jit(solution)/shard_map/ppermute | solution.py:75
  602.7 19.0 %collective-permute-start.61 = (f32[1,64,16,16]{1,3,2,0:T(8,128)S(1)}, f32[1,64,16,16]{1,3,2,0:T(8,128)S(1)}, u32[]{:S(2)}, u32[]{:S(2)}) collective-permute-start(f32[1,64,16,16]{1,3,2,0:T(8,128)S(1)} %get-tuple-element.40), channel_id=1, source_target_pairs={{0,5},{1,4},{2,7},{3,6},{4,1},{5,0},{6,3},{7,2},{8,13},{9,12},{10,... | collective-permute-start | bytes 196616 | tf_op jit(solution)/shard_map/ppermute | solution.py:75
  621.7 19.0 %collective-permute-start.62 = (f32[1,64,16,16]{1,3,2,0:T(8,128)S(1)}, f32[1,64,16,16]{1,3,2,0:T(8,128)S(1)}, u32[]{:S(2)}, u32[]{:S(2)}) collective-permute-start(f32[1,64,16,16]{1,3,2,0:T(8,128)S(1)} %get-tuple-element.39), channel_id=1, source_target_pairs={{0,6},{1,7},{2,4},{3,5},{4,2},{5,3},{6,0},{7,1},{8,14},{9,15},{10,... | collective-permute-start | bytes 196616 | tf_op jit(solution)/shard_map/ppermute | solution.py:75
  640.7 19.0 %collective-permute-start.63 = (f32[1,64,16,16]{1,3,2,0:T(8,128)S(1)}, f32[1,64,16,16]{1,3,2,0:T(8,128)S(1)}, u32[]{:S(2)}, u32[]{:S(2)}) collective-permute-start(f32[1,64,16,16]{1,3,2,0:T(8,128)S(1)} %get-tuple-element.38), channel_id=1, source_target_pairs={{0,7},{1,6},{2,5},{3,4},{4,3},{5,2},{6,1},{7,0},{8,15},{9,14},{10,... | collective-permute-start | bytes 196616 | tf_op jit(solution)/shard_map/ppermute | solution.py:75
  659.9 5.9 collective-permute-done.63
  666.6 7.4 constant_dynamic-slice_fusion.16
  678.6 8.6 collective-permute-start.65
  699.5 3.1 collective-permute-start.69
  716.6 4.4 collective-permute-start.73
  733.1 2.5 collective-permute-start.77
  737.5 2.9 collective-permute-start.79
  772.4 2.3 constant_dynamic-update-slice_fusion.25
  785.9 2.3 constant_dynamic-update-slice_fusion.18
  790.4 2.3 constant_dynamic-update-slice_fusion.16
  792.7 7.8 constant_dynamic-slice_fusion
  802.2 5.5 collective-permute-start.80
  809.3 4.8 collective-permute-start.81
  815.7 6.4 collective-permute-start.82
  823.7 7.8 collective-permute-start.83
  833.2 8.7 collective-permute-start.84
  843.5 11.9 %collective-permute-start.85 = (f32[1,1,128,16]{2,3,1,0:T(8,128)S(1)}, f32[1,1,128,16]{2,3,1,0:T(8,128)S(1)}, u32[]{:S(2)}, u32[]{:S(2)}) collective-permute-start(f32[1,1,128,16]{2,3,1,0:T(8,128)S(1)} %bitcast.376), channel_id=1, source_target_pairs={{48,0},{56,8},{64,16},{72,24},{80,32},{88,40},{96,48},{104,56},{11... | collective-permute-start | bytes 24584 | tf_op jit(solution)/shard_map/ppermute | solution.py:38
  863.6 9.7 collective-permute-start.86
  873.3 12.4 %collective-permute-start.87 = (f32[1,1,128,16]{2,3,1,0:T(8,128)S(1)}, f32[1,1,128,16]{2,3,1,0:T(8,128)S(1)}, u32[]{:S(2)}, u32[]{:S(2)}) collective-permute-start(f32[1,1,128,16]{2,3,1,0:T(8,128)S(1)} %bitcast.357), channel_id=1, source_target_pairs={{64,0},{72,8},{80,16},{88,24},{96,32},{104,40},{112,48},{120,56},{... | collective-permute-start | bytes 24584 | tf_op jit(solution)/shard_map/ppermute | solution.py:38
  885.7 10.1 %collective-permute-start.88 = (f32[1,1,128,16]{2,3,1,0:T(8,128)S(1)}, f32[1,1,128,16]{2,3,1,0:T(8,128)S(1)}, u32[]{:S(2)}, u32[]{:S(2)}) collective-permute-start(f32[1,1,128,16]{2,3,1,0:T(8,128)S(1)} %bitcast.353), channel_id=1, source_target_pairs={{72,0},{80,8},{88,16},{96,24},{104,32},{112,40},{120,48},{128,56},... | collective-permute-start | bytes 24584 | tf_op jit(solution)/shard_map/ppermute | solution.py:38
  946.1 2.3 constant_dynamic-update-slice_fusion.10
  967.5 19.0 %copy.524 = f32[33,1,1,128,16]{3,4,0,2,1:T(8,128)S(1)} copy(f32[33,1,1,128,16]{1,4,3,2,0:T(8,128)} %constant_dynamic-update-slice_fusion) | data formatting | bytes 540672 | tf_op jit(solution)/shard_map/stack | solution.py:96
  (368 shorter events, 361.6 us)
Async XLA Ops:
  21.9 64.2 %collective-permute-start.6 = (f32[1,64,16,16]{1,3,2,0:T(8,128)S(1)}, f32[1,64,16,16]{1,3,2,0:T(8,128)S(1)}, u32[]{:S(2)}, u32[]{:S(2)}) collective-permute-start(f32[1,64,16,16]{1,3,2,0:T(8,128)S(1)} %get-tuple-element.102), channel_id=1, source_target_pairs={{0,1},{1,0},{2,3},{3,2},{4,5},{5,4},{6,7},{7,6},{8,9},{9,8},{10,11... | collective-permute-start | bytes 196616 | tf_op jit(solution)/shard_map/ppermute | solution.py:75
  23.8 81.3 %collective-permute-start.7 = (f32[1,64,16,16]{1,3,2,0:T(8,128)S(1)}, f32[1,64,16,16]{1,3,2,0:T(8,128)S(1)}, u32[]{:S(2)}, u32[]{:S(2)}) collective-permute-start(f32[1,64,16,16]{1,3,2,0:T(8,128)S(1)} %get-tuple-element.101), channel_id=1, source_target_pairs={{0,2},{1,3},{2,0},{3,1},{4,6},{5,7},{6,4},{7,5},{8,10},{9,11},{10,... | collective-permute-start | bytes 196616 | tf_op jit(solution)/shard_map/ppermute | solution.py:75
  25.7 98.4 %collective-permute-start.8 = (f32[1,64,16,16]{1,3,2,0:T(8,128)S(1)}, f32[1,64,16,16]{1,3,2,0:T(8,128)S(1)}, u32[]{:S(2)}, u32[]{:S(2)}) collective-permute-start(f32[1,64,16,16]{1,3,2,0:T(8,128)S(1)} %get-tuple-element.100), channel_id=1, source_target_pairs={{0,3},{1,2},{2,1},{3,0},{4,7},{5,6},{6,5},{7,4},{8,11},{9,10},{10,... | collective-permute-start | bytes 196616 | tf_op jit(solution)/shard_map/ppermute | solution.py:75
  48.0 76.2 %collective-permute-start.9 = (f32[1,64,16,16]{1,3,2,0:T(8,128)S(1)}, f32[1,64,16,16]{1,3,2,0:T(8,128)S(1)}, u32[]{:S(2)}, u32[]{:S(2)}) collective-permute-start(f32[1,64,16,16]{1,3,2,0:T(8,128)S(1)} %get-tuple-element.99), channel_id=1, source_target_pairs={{0,4},{1,5},{2,6},{3,7},{4,0},{5,1},{6,2},{7,3},{8,12},{9,13},{10,... | collective-permute-start | bytes 196616 | tf_op jit(solution)/shard_map/ppermute | solution.py:75
  67.0 57.2 %collective-permute-start.10 = (f32[1,64,16,16]{1,3,2,0:T(8,128)S(1)}, f32[1,64,16,16]{1,3,2,0:T(8,128)S(1)}, u32[]{:S(2)}, u32[]{:S(2)}) collective-permute-start(f32[1,64,16,16]{1,3,2,0:T(8,128)S(1)} %get-tuple-element.98), channel_id=1, source_target_pairs={{0,5},{1,4},{2,7},{3,6},{4,1},{5,0},{6,3},{7,2},{8,13},{9,12},{10,... | collective-permute-start | bytes 196616 | tf_op jit(solution)/shard_map/ppermute | solution.py:75
  86.0 38.2 %collective-permute-start.11 = (f32[1,64,16,16]{1,3,2,0:T(8,128)S(1)}, f32[1,64,16,16]{1,3,2,0:T(8,128)S(1)}, u32[]{:S(2)}, u32[]{:S(2)}) collective-permute-start(f32[1,64,16,16]{1,3,2,0:T(8,128)S(1)} %get-tuple-element.97), channel_id=1, source_target_pairs={{0,6},{1,7},{2,4},{3,5},{4,2},{5,3},{6,0},{7,1},{8,14},{9,15},{10,... | collective-permute-start | bytes 196616 | tf_op jit(solution)/shard_map/ppermute | solution.py:75
  105.1 25.0 %collective-permute-start.12 = (f32[1,64,16,16]{1,3,2,0:T(8,128)S(1)}, f32[1,64,16,16]{1,3,2,0:T(8,128)S(1)}, u32[]{:S(2)}, u32[]{:S(2)}) collective-permute-start(f32[1,64,16,16]{1,3,2,0:T(8,128)S(1)} %get-tuple-element.96), channel_id=1, source_target_pairs={{0,7},{1,6},{2,5},{3,4},{4,3},{5,2},{6,1},{7,0},{8,15},{9,14},{10,... | collective-permute-start | bytes 196616 | tf_op jit(solution)/shard_map/ppermute | solution.py:75
  140.8 41.6 %collective-permute-start.33 = (f32[1,1,128,16]{2,3,1,0:T(8,128)S(1)}, f32[1,1,128,16]{2,3,1,0:T(8,128)S(1)}, u32[]{:S(2)}, u32[]{:S(2)}) collective-permute-start(f32[1,1,128,16]{2,3,1,0:T(8,128)S(1)} %bitcast.387), channel_id=1, source_target_pairs={{16,0},{24,8},{32,16},{40,24},{48,32},{56,40},{64,48},{72,56},{80,... | collective-permute-start | bytes 24584 | tf_op jit(solution)/shard_map/ppermute | solution.py:38
  151.9 36.1 %collective-permute-start.34 = (f32[1,1,128,16]{2,3,1,0:T(8,128)S(1)}, f32[1,1,128,16]{2,3,1,0:T(8,128)S(1)}, u32[]{:S(2)}, u32[]{:S(2)}) collective-permute-start(f32[1,1,128,16]{2,3,1,0:T(8,128)S(1)} %bitcast.386), channel_id=1, source_target_pairs={{24,0},{32,8},{40,16},{48,24},{56,32},{64,40},{72,48},{80,56},{88,... | collective-permute-start | bytes 24584 | tf_op jit(solution)/shard_map/ppermute | solution.py:38
  159.1 37.2 %collective-permute-start.35 = (f32[1,1,128,16]{2,3,1,0:T(8,128)S(1)}, f32[1,1,128,16]{2,3,1,0:T(8,128)S(1)}, u32[]{:S(2)}, u32[]{:S(2)}) collective-permute-start(f32[1,1,128,16]{2,3,1,0:T(8,128)S(1)} %bitcast.385), channel_id=1, source_target_pairs={{32,0},{40,8},{48,16},{56,24},{64,32},{72,40},{80,48},{88,56},{96,... | collective-permute-start | bytes 24584 | tf_op jit(solution)/shard_map/ppermute | solution.py:38
  164.9 44.0 %collective-permute-start.36 = (f32[1,1,128,16]{2,3,1,0:T(8,128)S(1)}, f32[1,1,128,16]{2,3,1,0:T(8,128)S(1)}, u32[]{:S(2)}, u32[]{:S(2)}) collective-permute-start(f32[1,1,128,16]{2,3,1,0:T(8,128)S(1)} %bitcast.373), channel_id=1, source_target_pairs={{40,0},{48,8},{56,16},{64,24},{72,32},{80,40},{88,48},{96,56},{104... | collective-permute-start | bytes 24584 | tf_op jit(solution)/shard_map/ppermute | solution.py:38
  168.4 42.3 %collective-permute-start.37 = (f32[1,1,128,16]{2,3,1,0:T(8,128)S(1)}, f32[1,1,128,16]{2,3,1,0:T(8,128)S(1)}, u32[]{:S(2)}, u32[]{:S(2)}) collective-permute-start(f32[1,1,128,16]{2,3,1,0:T(8,128)S(1)} %bitcast.371), channel_id=1, source_target_pairs={{48,0},{56,8},{64,16},{72,24},{80,32},{88,40},{96,48},{104,56},{11... | collective-permute-start | bytes 24584 | tf_op jit(solution)/shard_map/ppermute | solution.py:38
  182.4 30.3 %collective-permute-start.38 = (f32[1,1,128,16]{2,3,1,0:T(8,128)S(1)}, f32[1,1,128,16]{2,3,1,0:T(8,128)S(1)}, u32[]{:S(2)}, u32[]{:S(2)}) collective-permute-start(f32[1,1,128,16]{2,3,1,0:T(8,128)S(1)} %bitcast.369), channel_id=1, source_target_pairs={{56,0},{64,8},{72,16},{80,24},{88,32},{96,40},{104,48},{112,56},{1... | collective-permute-start | bytes 24584 | tf_op jit(solution)/shard_map/ppermute | solution.py:38
  188.1 26.5 %collective-permute-start.39 = (f32[1,1,128,16]{2,3,1,0:T(8,128)S(1)}, f32[1,1,128,16]{2,3,1,0:T(8,128)S(1)}, u32[]{:S(2)}, u32[]{:S(2)}) collective-permute-start(f32[1,1,128,16]{2,3,1,0:T(8,128)S(1)} %bitcast.361), channel_id=1, source_target_pairs={{64,0},{72,8},{80,16},{88,24},{96,32},{104,40},{112,48},{120,56},{... | collective-permute-start | bytes 24584 | tf_op jit(solution)/shard_map/ppermute | solution.py:38
  214.6 24.2 %collective-permute-start.44 = (f32[1,1,128,16]{2,3,1,0:T(8,128)S(1)}, f32[1,1,128,16]{2,3,1,0:T(8,128)S(1)}, u32[]{:S(2)}, u32[]{:S(2)}) collective-permute-start(f32[1,1,128,16]{2,3,1,0:T(8,128)S(1)} %bitcast.289), channel_id=1, source_target_pairs={{104,0},{112,8},{120,16},{128,24},{136,32},{144,40},{152,48},{160,... | collective-permute-start | bytes 24584 | tf_op jit(solution)/shard_map/ppermute | solution.py:38
  216.6 41.3 %collective-permute-start.45 = (f32[1,1,128,16]{2,3,1,0:T(8,128)S(1)}, f32[1,1,128,16]{2,3,1,0:T(8,128)S(1)}, u32[]{:S(2)}, u32[]{:S(2)}) collective-permute-start(f32[1,1,128,16]{2,3,1,0:T(8,128)S(1)} %bitcast.288), channel_id=1, source_target_pairs={{112,0},{120,8},{128,16},{136,24},{144,32},{152,40},{160,48},{168,... | collective-permute-start | bytes 24584 | tf_op jit(solution)/shard_map/ppermute | solution.py:38
  224.3 69.1 %collective-permute-start.46 = (f32[1,1,128,16]{2,3,1,0:T(8,128)S(1)}, f32[1,1,128,16]{2,3,1,0:T(8,128)S(1)}, u32[]{:S(2)}, u32[]{:S(2)}) collective-permute-start(f32[1,1,128,16]{2,3,1,0:T(8,128)S(1)} %bitcast.343), channel_id=1, source_target_pairs={{120,0},{128,8},{136,16},{144,24},{152,32},{160,40},{168,48},{176,... | collective-permute-start | bytes 24584 | tf_op jit(solution)/shard_map/ppermute | solution.py:38
  226.2 68.5 %collective-permute-start.47 = (f32[1,1,128,16]{2,3,1,0:T(8,128)S(1)}, f32[1,1,128,16]{2,3,1,0:T(8,128)S(1)}, u32[]{:S(2)}, u32[]{:S(2)}) collective-permute-start(f32[1,1,128,16]{2,3,1,0:T(8,128)S(1)} %bitcast.333), channel_id=1, source_target_pairs={{128,0},{136,8},{144,16},{152,24},{160,32},{168,40},{176,48},{184,... | collective-permute-start | bytes 24584 | tf_op jit(solution)/shard_map/ppermute | solution.py:38
  227.5 75.8 %collective-permute-start.48 = (f32[1,1,128,16]{2,3,1,0:T(8,128)S(1)}, f32[1,1,128,16]{2,3,1,0:T(8,128)S(1)}, u32[]{:S(2)}, u32[]{:S(2)}) collective-permute-start(f32[1,1,128,16]{2,3,1,0:T(8,128)S(1)} %bitcast.325), channel_id=1, source_target_pairs={{136,0},{144,8},{152,16},{160,24},{168,32},{176,40},{184,48},{192,... | collective-permute-start | bytes 24584 | tf_op jit(solution)/shard_map/ppermute | solution.py:38
  238.8 66.5 %collective-permute-start.49 = (f32[1,1,128,16]{2,3,1,0:T(8,128)S(1)}, f32[1,1,128,16]{2,3,1,0:T(8,128)S(1)}, u32[]{:S(2)}, u32[]{:S(2)}) collective-permute-start(f32[1,1,128,16]{2,3,1,0:T(8,128)S(1)} %bitcast.319), channel_id=1, source_target_pairs={{144,0},{152,8},{160,16},{168,24},{176,32},{184,40},{192,48},{200,... | collective-permute-start | bytes 24584 | tf_op jit(solution)/shard_map/ppermute | solution.py:38
  257.8 49.4 %collective-permute-start.50 = (f32[1,1,128,16]{2,3,1,0:T(8,128)S(1)}, f32[1,1,128,16]{2,3,1,0:T(8,128)S(1)}, u32[]{:S(2)}, u32[]{:S(2)}) collective-permute-start(f32[1,1,128,16]{2,3,1,0:T(8,128)S(1)} %bitcast.316), channel_id=1, source_target_pairs={{152,0},{160,8},{168,16},{176,24},{184,32},{192,40},{200,48},{208,... | collective-permute-start | bytes 24584 | tf_op jit(solution)/shard_map/ppermute | solution.py:38
  293.4 23.9 %collective-permute-start.16 = (f32[1,1,128,16]{2,3,1,0:T(8,128)S(1)}, f32[1,1,128,16]{2,3,1,0:T(8,128)S(1)}, u32[]{:S(2)}, u32[]{:S(2)}) collective-permute-start(f32[1,1,128,16]{2,3,1,0:T(8,128)S(1)} %bitcast.363), channel_id=1, source_target_pairs={{0,128},{8,136},{16,144},{24,152},{32,160},{40,168},{48,176},{56,1... | collective-permute-start | bytes 24584 | tf_op jit(solution)/shard_map/ppermute | solution.py:38
  294.7 25.7 %collective-permute-start.17 = (f32[1,1,128,16]{2,3,1,0:T(8,128)S(1)}, f32[1,1,128,16]{2,3,1,0:T(8,128)S(1)}, u32[]{:S(2)}, u32[]{:S(2)}) collective-permute-start(f32[1,1,128,16]{2,3,1,0:T(8,128)S(1)} %bitcast.356), channel_id=1, source_target_pairs={{0,120},{8,128},{16,136},{24,144},{32,152},{40,160},{48,168},{56,1... | collective-permute-start | bytes 24584 | tf_op jit(solution)/shard_map/ppermute | solution.py:38
  317.3 25.4 %collective-permute-start.21 = (f32[1,1,128,16]{2,3,1,0:T(8,128)S(1)}, f32[1,1,128,16]{2,3,1,0:T(8,128)S(1)}, u32[]{:S(2)}, u32[]{:S(2)}) collective-permute-start(f32[1,1,128,16]{2,3,1,0:T(8,128)S(1)} %bitcast.334), channel_id=1, source_target_pairs={{0,88},{8,96},{16,104},{24,112},{32,120},{40,128},{48,136},{56,144... | collective-permute-start | bytes 24584 | tf_op jit(solution)/shard_map/ppermute | solution.py:38
  320.5 24.2 %collective-permute-start.22 = (f32[1,1,128,16]{2,3,1,0:T(8,128)S(1)}, f32[1,1,128,16]{2,3,1,0:T(8,128)S(1)}, u32[]{:S(2)}, u32[]{:S(2)}) collective-permute-start(f32[1,1,128,16]{2,3,1,0:T(8,128)S(1)} %bitcast.326), channel_id=1, source_target_pairs={{0,80},{8,88},{16,96},{24,104},{32,112},{40,120},{48,128},{56,136}... | collective-permute-start | bytes 24584 | tf_op jit(solution)/shard_map/ppermute | solution.py:38
  322.4 24.2 %collective-permute-start.23 = (f32[1,1,128,16]{2,3,1,0:T(8,128)S(1)}, f32[1,1,128,16]{2,3,1,0:T(8,128)S(1)}, u32[]{:S(2)}, u32[]{:S(2)}) collective-permute-start(f32[1,1,128,16]{2,3,1,0:T(8,128)S(1)} %bitcast.320), channel_id=1, source_target_pairs={{0,72},{8,80},{16,88},{24,96},{32,104},{40,112},{48,120},{56,128},... | collective-permute-start | bytes 24584 | tf_op jit(solution)/shard_map/ppermute | solution.py:38
  324.3 24.2 %collective-permute-start.24 = (f32[1,1,128,16]{2,3,1,0:T(8,128)S(1)}, f32[1,1,128,16]{2,3,1,0:T(8,128)S(1)}, u32[]{:S(2)}, u32[]{:S(2)}) collective-permute-start(f32[1,1,128,16]{2,3,1,0:T(8,128)S(1)} %bitcast.315), channel_id=1, source_target_pairs={{0,64},{8,72},{16,80},{24,88},{32,96},{40,104},{48,112},{56,120},{... | collective-permute-start | bytes 24584 | tf_op jit(solution)/shard_map/ppermute | solution.py:38
  326.3 24.8 %collective-permute-start.25 = (f32[1,1,128,16]{2,3,1,0:T(8,128)S(1)}, f32[1,1,128,16]{2,3,1,0:T(8,128)S(1)}, u32[]{:S(2)}, u32[]{:S(2)}) collective-permute-start(f32[1,1,128,16]{2,3,1,0:T(8,128)S(1)} %bitcast.314), channel_id=1, source_target_pairs={{0,56},{8,64},{16,72},{24,80},{32,88},{40,96},{48,104},{56,112},{6... | collective-permute-start | bytes 24584 | tf_op jit(solution)/shard_map/ppermute | solution.py:38
  346.6 23.9 %collective-permute-start.28 = (f32[1,1,128,16]{2,3,1,0:T(8,128)}, f32[1,1,128,16]{2,3,1,0:T(8,128)S(1)}, u32[]{:S(2)}, u32[]{:S(2)}) collective-permute-start(f32[1,1,128,16]{2,3,1,0:T(8,128)} %bitcast.66), channel_id=1, source_target_pairs={{0,32},{8,40},{16,48},{24,56},{32,64},{40,72},{48,80},{56,88},{64,... | collective-permute-start | bytes 24584 | tf_op jit(solution)/shard_map/ppermute | solution.py:38
  348.6 56.9 %collective-permute-start.29 = (f32[1,1,128,16]{2,3,1,0:T(8,128)}, f32[1,1,128,16]{2,3,1,0:T(8,128)S(1)}, u32[]{:S(2)}, u32[]{:S(2)}) collective-permute-start(f32[1,1,128,16]{2,3,1,0:T(8,128)} %bitcast.68), channel_id=1, source_target_pairs={{0,24},{8,32},{16,40},{24,48},{32,56},{40,64},{48,72},{56,80},{64,... | collective-permute-start | bytes 24584 | tf_op jit(solution)/shard_map/ppermute | solution.py:38
  351.0 73.5 %collective-permute-start.30 = (f32[1,1,128,16]{2,3,1,0:T(8,128)}, f32[1,1,128,16]{2,3,1,0:T(8,128)S(1)}, u32[]{:S(2)}, u32[]{:S(2)}) collective-permute-start(f32[1,1,128,16]{2,3,1,0:T(8,128)} %bitcast.70), channel_id=1, source_target_pairs={{0,16},{8,24},{16,32},{24,40},{32,48},{40,56},{48,64},{56,72},{64,... | collective-permute-start | bytes 24584 | tf_op jit(solution)/shard_map/ppermute | solution.py:38
  362.5 137.0 %collective-permute-start.31 = (f32[1,1,128,16]{2,3,1,0:T(8,128)S(1)}, f32[1,1,128,16]{2,3,1,0:T(8,128)}, u32[]{:S(2)}, u32[]{:S(2)}) collective-permute-start(f32[1,1,128,16]{2,3,1,0:T(8,128)S(1)} %bitcast.309), channel_id=1, source_target_pairs={{0,8},{8,16},{16,24},{24,32},{32,40},{40,48},{48,56},{56,64},{64,7... | collective-permute-start | bytes 24584 | tf_op jit(solution)/shard_map/ppermute | solution.py:38
  365.0 136.6 %collective-permute-start.32 = (f32[1,1,128,16]{2,3,1,0:T(8,128)S(1)}, f32[1,1,128,16]{2,3,1,0:T(8,128)}, u32[]{:S(2)}, u32[]{:S(2)}) collective-permute-start(f32[1,1,128,16]{2,3,1,0:T(8,128)S(1)} %bitcast.306), channel_id=1, source_target_pairs={{8,0},{16,8},{24,16},{32,24},{40,32},{48,40},{56,48},{64,56},{72,6... | collective-permute-start | bytes 24584 | tf_op jit(solution)/shard_map/ppermute | solution.py:38
  370.5 133.2 %collective-permute-start.13 = (f32[1,1,128,16]{2,3,1,0:T(8,128)S(1)}, f32[1,1,128,16]{2,3,1,0:T(8,128)}, u32[]{:S(2)}, u32[]{:S(2)}) collective-permute-start(f32[1,1,128,16]{2,3,1,0:T(8,128)S(1)} %bitcast.303), channel_id=1, source_target_pairs={{0,152},{8,160},{16,168},{24,176},{32,184},{40,192},{48,200},{56,2... | collective-permute-start | bytes 24584 | tf_op jit(solution)/shard_map/ppermute | solution.py:38
  405.5 100.2 %collective-permute-start.14 = (f32[1,1,128,16]{2,3,1,0:T(8,128)S(1)}, f32[1,1,128,16]{2,3,1,0:T(8,128)}, u32[]{:S(2)}, u32[]{:S(2)}) collective-permute-start(f32[1,1,128,16]{2,3,1,0:T(8,128)S(1)} %bitcast.299), channel_id=1, source_target_pairs={{0,144},{8,152},{16,160},{24,168},{32,176},{40,184},{48,192},{56,2... | collective-permute-start | bytes 24584 | tf_op jit(solution)/shard_map/ppermute | solution.py:38
  424.5 83.3 %collective-permute-start.15 = (f32[1,1,128,16]{2,3,1,0:T(8,128)S(1)}, f32[1,1,128,16]{2,3,1,0:T(8,128)}, u32[]{:S(2)}, u32[]{:S(2)}) collective-permute-start(f32[1,1,128,16]{2,3,1,0:T(8,128)S(1)} %bitcast.297), channel_id=1, source_target_pairs={{0,136},{8,144},{16,152},{24,160},{32,168},{40,176},{48,184},{56,1... | collective-permute-start | bytes 24584 | tf_op jit(solution)/shard_map/ppermute | solution.py:38
  558.3 63.4 %collective-permute-start.57 = (f32[1,64,16,16]{1,3,2,0:T(8,128)S(1)}, f32[1,64,16,16]{1,3,2,0:T(8,128)S(1)}, u32[]{:S(2)}, u32[]{:S(2)}) collective-permute-start(f32[1,64,16,16]{1,3,2,0:T(8,128)S(1)} %get-tuple-element.44), channel_id=1, source_target_pairs={{0,1},{1,0},{2,3},{3,2},{4,5},{5,4},{6,7},{7,6},{8,9},{9,8},{10,11... | collective-permute-start | bytes 196616 | tf_op jit(solution)/shard_map/ppermute | solution.py:75
  560.2 80.5 %collective-permute-start.58 = (f32[1,64,16,16]{1,3,2,0:T(8,128)S(1)}, f32[1,64,16,16]{1,3,2,0:T(8,128)S(1)}, u32[]{:S(2)}, u32[]{:S(2)}) collective-permute-start(f32[1,64,16,16]{1,3,2,0:T(8,128)S(1)} %get-tuple-element.43), channel_id=1, source_target_pairs={{0,2},{1,3},{2,0},{3,1},{4,6},{5,7},{6,4},{7,5},{8,10},{9,11},{10,... | collective-permute-start | bytes 196616 | tf_op jit(solution)/shard_map/ppermute | solution.py:75
  562.2 97.6 %collective-permute-start.59 = (f32[1,64,16,16]{1,3,2,0:T(8,128)S(1)}, f32[1,64,16,16]{1,3,2,0:T(8,128)S(1)}, u32[]{:S(2)}, u32[]{:S(2)}) collective-permute-start(f32[1,64,16,16]{1,3,2,0:T(8,128)S(1)} %get-tuple-element.42), channel_id=1, source_target_pairs={{0,3},{1,2},{2,1},{3,0},{4,7},{5,6},{6,5},{7,4},{8,11},{9,10},{10,... | collective-permute-start | bytes 196616 | tf_op jit(solution)/shard_map/ppermute | solution.py:75
  583.6 76.2 %collective-permute-start.60 = (f32[1,64,16,16]{1,3,2,0:T(8,128)S(1)}, f32[1,64,16,16]{1,3,2,0:T(8,128)S(1)}, u32[]{:S(2)}, u32[]{:S(2)}) collective-permute-start(f32[1,64,16,16]{1,3,2,0:T(8,128)S(1)} %get-tuple-element.41), channel_id=1, source_target_pairs={{0,4},{1,5},{2,6},{3,7},{4,0},{5,1},{6,2},{7,3},{8,12},{9,13},{10,... | collective-permute-start | bytes 196616 | tf_op jit(solution)/shard_map/ppermute | solution.py:75
  602.7 57.2 %collective-permute-start.61 = (f32[1,64,16,16]{1,3,2,0:T(8,128)S(1)}, f32[1,64,16,16]{1,3,2,0:T(8,128)S(1)}, u32[]{:S(2)}, u32[]{:S(2)}) collective-permute-start(f32[1,64,16,16]{1,3,2,0:T(8,128)S(1)} %get-tuple-element.40), channel_id=1, source_target_pairs={{0,5},{1,4},{2,7},{3,6},{4,1},{5,0},{6,3},{7,2},{8,13},{9,12},{10,... | collective-permute-start | bytes 196616 | tf_op jit(solution)/shard_map/ppermute | solution.py:75
  621.7 38.2 %collective-permute-start.62 = (f32[1,64,16,16]{1,3,2,0:T(8,128)S(1)}, f32[1,64,16,16]{1,3,2,0:T(8,128)S(1)}, u32[]{:S(2)}, u32[]{:S(2)}) collective-permute-start(f32[1,64,16,16]{1,3,2,0:T(8,128)S(1)} %get-tuple-element.39), channel_id=1, source_target_pairs={{0,6},{1,7},{2,4},{3,5},{4,2},{5,3},{6,0},{7,1},{8,14},{9,15},{10,... | collective-permute-start | bytes 196616 | tf_op jit(solution)/shard_map/ppermute | solution.py:75
  640.7 25.0 %collective-permute-start.63 = (f32[1,64,16,16]{1,3,2,0:T(8,128)S(1)}, f32[1,64,16,16]{1,3,2,0:T(8,128)S(1)}, u32[]{:S(2)}, u32[]{:S(2)}) collective-permute-start(f32[1,64,16,16]{1,3,2,0:T(8,128)S(1)} %get-tuple-element.38), channel_id=1, source_target_pairs={{0,7},{1,6},{2,5},{3,4},{4,3},{5,2},{6,1},{7,0},{8,15},{9,14},{10,... | collective-permute-start | bytes 196616 | tf_op jit(solution)/shard_map/ppermute | solution.py:75
  675.6 23.8 %collective-permute-start.64 = (f32[1,1,128,16]{2,3,1,0:T(8,128)S(1)}, f32[1,1,128,16]{2,3,1,0:T(8,128)S(1)}, u32[]{:S(2)}, u32[]{:S(2)}) collective-permute-start(f32[1,1,128,16]{2,3,1,0:T(8,128)S(1)} %bitcast.388), channel_id=1, source_target_pairs={{0,128},{8,136},{16,144},{24,152},{32,160},{40,168},{48,176},{56,1... | collective-permute-start | bytes 24584 | tf_op jit(solution)/shard_map/ppermute | solution.py:38
  678.6 32.2 %collective-permute-start.65 = (f32[1,1,128,16]{2,3,1,0:T(8,128)S(1)}, f32[1,1,128,16]{2,3,1,0:T(8,128)S(1)}, u32[]{:S(2)}, u32[]{:S(2)}) collective-permute-start(f32[1,1,128,16]{2,3,1,0:T(8,128)S(1)} %bitcast.383), channel_id=1, source_target_pairs={{0,120},{8,128},{16,136},{24,144},{32,152},{40,160},{48,168},{56,1... | collective-permute-start | bytes 24584 | tf_op jit(solution)/shard_map/ppermute | solution.py:38
  688.8 23.9 %collective-permute-start.66 = (f32[1,1,128,16]{2,3,1,0:T(8,128)S(1)}, f32[1,1,128,16]{2,3,1,0:T(8,128)S(1)}, u32[]{:S(2)}, u32[]{:S(2)}) collective-permute-start(f32[1,1,128,16]{2,3,1,0:T(8,128)S(1)} %bitcast.381), channel_id=1, source_target_pairs={{0,112},{8,120},{16,128},{24,136},{32,144},{40,152},{48,160},{56,1... | collective-permute-start | bytes 24584 | tf_op jit(solution)/shard_map/ppermute | solution.py:38
  692.4 22.3 %collective-permute-start.67 = (f32[1,1,128,16]{2,3,1,0:T(8,128)S(1)}, f32[1,1,128,16]{2,3,1,0:T(8,128)S(1)}, u32[]{:S(2)}, u32[]{:S(2)}) collective-permute-start(f32[1,1,128,16]{2,3,1,0:T(8,128)S(1)} %bitcast.379), channel_id=1, source_target_pairs={{0,104},{8,112},{16,120},{24,128},{32,136},{40,144},{48,152},{56,1... | collective-permute-start | bytes 24584 | tf_op jit(solution)/shard_map/ppermute | solution.py:38
  699.5 21.5 %collective-permute-start.69 = (f32[1,1,128,16]{2,3,1,0:T(8,128)S(1)}, f32[1,1,128,16]{2,3,1,0:T(8,128)S(1)}, u32[]{:S(2)}, u32[]{:S(2)}) collective-permute-start(f32[1,1,128,16]{2,3,1,0:T(8,128)S(1)} %bitcast.374), channel_id=1, source_target_pairs={{0,88},{8,96},{16,104},{24,112},{32,120},{40,128},{48,136},{56,144... | collective-permute-start | bytes 24584 | tf_op jit(solution)/shard_map/ppermute | solution.py:38
  729.2 24.7 %collective-permute-start.75 = (f32[1,1,128,16]{2,3,1,0:T(8,128)S(1)}, f32[1,1,128,16]{2,3,1,0:T(8,128)S(1)}, u32[]{:S(2)}, u32[]{:S(2)}) collective-permute-start(f32[1,1,128,16]{2,3,1,0:T(8,128)S(1)} %bitcast.351), channel_id=1, source_target_pairs={{0,40},{8,48},{16,56},{24,64},{32,72},{40,80},{48,88},{56,96},{64,... | collective-permute-start | bytes 24584 | tf_op jit(solution)/shard_map/ppermute | solution.py:38
  731.1 24.2 %collective-permute-start.76 = (f32[1,1,128,16]{2,3,1,0:T(8,128)S(1)}, f32[1,1,128,16]{2,3,1,0:T(8,128)S(1)}, u32[]{:S(2)}, u32[]{:S(2)}) collective-permute-start(f32[1,1,128,16]{2,3,1,0:T(8,128)S(1)} %bitcast.344), channel_id=1, source_target_pairs={{0,32},{8,40},{16,48},{24,56},{32,64},{40,72},{48,80},{56,88},{64,... | collective-permute-start | bytes 24584 | tf_op jit(solution)/shard_map/ppermute | solution.py:38
  733.1 23.7 %collective-permute-start.77 = (f32[1,1,128,16]{2,3,1,0:T(8,128)S(1)}, f32[1,1,128,16]{2,3,1,0:T(8,128)S(1)}, u32[]{:S(2)}, u32[]{:S(2)}) collective-permute-start(f32[1,1,128,16]{2,3,1,0:T(8,128)S(1)} %bitcast.339), channel_id=1, source_target_pairs={{0,24},{8,32},{16,40},{24,48},{32,56},{40,64},{48,72},{56,80},{64,... | collective-permute-start | bytes 24584 | tf_op jit(solution)/shard_map/ppermute | solution.py:38
  735.6 22.6 %collective-permute-start.78 = (f32[1,1,128,16]{2,3,1,0:T(8,128)S(1)}, f32[1,1,128,16]{2,3,1,0:T(8,128)S(1)}, u32[]{:S(2)}, u32[]{:S(2)}) collective-permute-start(f32[1,1,128,16]{2,3,1,0:T(8,128)S(1)} %bitcast.332), channel_id=1, source_target_pairs={{0,16},{8,24},{16,32},{24,40},{32,48},{40,56},{48,64},{56,72},{64,... | collective-permute-start | bytes 24584 | tf_op jit(solution)/shard_map/ppermute | solution.py:38
  737.5 22.1 %collective-permute-start.79 = (f32[1,1,128,16]{2,3,1,0:T(8,128)S(1)}, f32[1,1,128,16]{2,3,1,0:T(8,128)S(1)}, u32[]{:S(2)}, u32[]{:S(2)}) collective-permute-start(f32[1,1,128,16]{2,3,1,0:T(8,128)S(1)} %bitcast.327), channel_id=1, source_target_pairs={{0,8},{8,16},{16,24},{24,32},{32,40},{40,48},{48,56},{56,64},{64,7... | collective-permute-start | bytes 24584 | tf_op jit(solution)/shard_map/ppermute | solution.py:38
  802.2 41.4 %collective-permute-start.80 = (f32[1,1,128,16]{2,3,1,0:T(8,128)S(1)}, f32[1,1,128,16]{2,3,1,0:T(8,128)S(1)}, u32[]{:S(2)}, u32[]{:S(2)}) collective-permute-start(f32[1,1,128,16]{2,3,1,0:T(8,128)S(1)} %bitcast.389), channel_id=1, source_target_pairs={{8,0},{16,8},{24,16},{32,24},{40,32},{48,40},{56,48},{64,56},{72,6... | collective-permute-start | bytes 24584 | tf_op jit(solution)/shard_map/ppermute | solution.py:38
  809.3 54.3 %collective-permute-start.81 = (f32[1,1,128,16]{2,3,1,0:T(8,128)S(1)}, f32[1,1,128,16]{2,3,1,0:T(8,128)S(1)}, u32[]{:S(2)}, u32[]{:S(2)}) collective-permute-start(f32[1,1,128,16]{2,3,1,0:T(8,128)S(1)} %bitcast.384), channel_id=1, source_target_pairs={{16,0},{24,8},{32,16},{40,24},{48,32},{56,40},{64,48},{72,56},{80,... | collective-permute-start | bytes 24584 | tf_op jit(solution)/shard_map/ppermute | solution.py:38
  815.7 57.6 %collective-permute-start.82 = (f32[1,1,128,16]{2,3,1,0:T(8,128)S(1)}, f32[1,1,128,16]{2,3,1,0:T(8,128)S(1)}, u32[]{:S(2)}, u32[]{:S(2)}) collective-permute-start(f32[1,1,128,16]{2,3,1,0:T(8,128)S(1)} %bitcast.382), channel_id=1, source_target_pairs={{24,0},{32,8},{40,16},{48,24},{56,32},{64,40},{72,48},{80,56},{88,... | collective-permute-start | bytes 24584 | tf_op jit(solution)/shard_map/ppermute | solution.py:38
  823.7 62.0 %collective-permute-start.83 = (f32[1,1,128,16]{2,3,1,0:T(8,128)S(1)}, f32[1,1,128,16]{2,3,1,0:T(8,128)S(1)}, u32[]{:S(2)}, u32[]{:S(2)}) collective-permute-start(f32[1,1,128,16]{2,3,1,0:T(8,128)S(1)} %bitcast.380), channel_id=1, source_target_pairs={{32,0},{40,8},{48,16},{56,24},{64,32},{72,40},{80,48},{88,56},{96,... | collective-permute-start | bytes 24584 | tf_op jit(solution)/shard_map/ppermute | solution.py:38
  833.2 62.6 %collective-permute-start.84 = (f32[1,1,128,16]{2,3,1,0:T(8,128)S(1)}, f32[1,1,128,16]{2,3,1,0:T(8,128)S(1)}, u32[]{:S(2)}, u32[]{:S(2)}) collective-permute-start(f32[1,1,128,16]{2,3,1,0:T(8,128)S(1)} %bitcast.378), channel_id=1, source_target_pairs={{40,0},{48,8},{56,16},{64,24},{72,32},{80,40},{88,48},{96,56},{104... | collective-permute-start | bytes 24584 | tf_op jit(solution)/shard_map/ppermute | solution.py:38
  843.5 54.4 %collective-permute-start.85 = (f32[1,1,128,16]{2,3,1,0:T(8,128)S(1)}, f32[1,1,128,16]{2,3,1,0:T(8,128)S(1)}, u32[]{:S(2)}, u32[]{:S(2)}) collective-permute-start(f32[1,1,128,16]{2,3,1,0:T(8,128)S(1)} %bitcast.376), channel_id=1, source_target_pairs={{48,0},{56,8},{64,16},{72,24},{80,32},{88,40},{96,48},{104,56},{11... | collective-permute-start | bytes 24584 | tf_op jit(solution)/shard_map/ppermute | solution.py:38
  863.6 42.0 %collective-permute-start.86 = (f32[1,1,128,16]{2,3,1,0:T(8,128)S(1)}, f32[1,1,128,16]{2,3,1,0:T(8,128)S(1)}, u32[]{:S(2)}, u32[]{:S(2)}) collective-permute-start(f32[1,1,128,16]{2,3,1,0:T(8,128)S(1)} %bitcast.365), channel_id=1, source_target_pairs={{56,0},{64,8},{72,16},{80,24},{88,32},{96,40},{104,48},{112,56},{1... | collective-permute-start | bytes 24584 | tf_op jit(solution)/shard_map/ppermute | solution.py:38
  873.3 34.2 %collective-permute-start.87 = (f32[1,1,128,16]{2,3,1,0:T(8,128)S(1)}, f32[1,1,128,16]{2,3,1,0:T(8,128)S(1)}, u32[]{:S(2)}, u32[]{:S(2)}) collective-permute-start(f32[1,1,128,16]{2,3,1,0:T(8,128)S(1)} %bitcast.357), channel_id=1, source_target_pairs={{64,0},{72,8},{80,16},{88,24},{96,32},{104,40},{112,48},{120,56},{... | collective-permute-start | bytes 24584 | tf_op jit(solution)/shard_map/ppermute | solution.py:38
  885.7 23.8 %collective-permute-start.88 = (f32[1,1,128,16]{2,3,1,0:T(8,128)S(1)}, f32[1,1,128,16]{2,3,1,0:T(8,128)S(1)}, u32[]{:S(2)}, u32[]{:S(2)}) collective-permute-start(f32[1,1,128,16]{2,3,1,0:T(8,128)S(1)} %bitcast.353), channel_id=1, source_target_pairs={{72,0},{80,8},{88,16},{96,24},{104,32},{112,40},{120,48},{128,56},... | collective-permute-start | bytes 24584 | tf_op jit(solution)/shard_map/ppermute | solution.py:38
  905.6 22.1 %collective-permute-start.91 = (f32[1,1,128,16]{2,3,1,0:T(8,128)S(1)}, f32[1,1,128,16]{2,3,1,0:T(8,128)S(1)}, u32[]{:S(2)}, u32[]{:S(2)}) collective-permute-start(f32[1,1,128,16]{2,3,1,0:T(8,128)S(1)} %bitcast.348), channel_id=1, source_target_pairs={{96,0},{104,8},{112,16},{120,24},{128,32},{136,40},{144,48},{152,5... | collective-permute-start | bytes 24584 | tf_op jit(solution)/shard_map/ppermute | solution.py:38
  907.6 21.5 %collective-permute-start.92 = (f32[1,1,128,16]{2,3,1,0:T(8,128)S(1)}, f32[1,1,128,16]{2,3,1,0:T(8,128)S(1)}, u32[]{:S(2)}, u32[]{:S(2)}) collective-permute-start(f32[1,1,128,16]{2,3,1,0:T(8,128)S(1)} %bitcast.340), channel_id=1, source_target_pairs={{104,0},{112,8},{120,16},{128,24},{136,32},{144,40},{152,48},{160,... | collective-permute-start | bytes 24584 | tf_op jit(solution)/shard_map/ppermute | solution.py:38
  (36 other events, 859.9 us)
